TPU v7x, 128 devices: a whole 4x4x4 slice. The times are simulated.
128 devices in a mesh: lat: 8 (over y_lo, x), lon: 16 (over y_hi, z, core).
Axes of the slice: x: 4, y: 4 (y_hi: 2, y_lo: 2; y = y_hi * 2 + y_lo), z: 4, core: 2. Of those that a mesh axis runs over, the one named last changes fastest.
Arguments:
- inputs: bfloat16 [64, 2, 2, 192, 2048], P(None, None, None, 'lat', 'lon'), may hold values from -6 to 6
- kernels: float32 [2, 9, 128], replicated, may hold values from -0.6 to 0.6
- w_down: bfloat16 [9, 128, 64], replicated, may hold values from -0.25 to 0.25
- w_up: bfloat16 [9, 64, 128], replicated, may hold values from -0.3125 to 0.3125
- cotangent: bfloat16 [64, 2, 2, 192, 2048], P(None, None, None, 'lat', 'lon'), may hold values from -6 to 6
- coverage: int32 [24, 256], P('lat', 'lon'), may hold values 0 or 1
Outputs:
- decoded: bfloat16 [64, 2, 2, 192, 2048], P(None, None, None, 'lat', 'lon')
- grad_input: bfloat16 [64, 2, 2, 192, 2048], P(None, None, None, 'lat', 'lon')
- grad_down: float32 [9, 128, 64], replicated
- grad_up: float32 [9, 64, 128], replicated
- grad_kernels: float32 [2, 9, 128], P(None, None, ('lat', 'lon'))
Inputs may be any that keep to these rules, and one draw needn't show every extreme that they name: 1 where the tile carries loss gradient, 0 where it has no swath coverage.
All inputs are finite; a program needn't handle non-finite values. No bound on the sum of `coverage` on one device may be relied on, other than what follows from the above.
Results may differ from a plain program's by a relative error of at most 0.012.
Values may be sent and summed in bfloat16 or wider, within the bound.
A program may use at most 128 MiB of HBM per device.

v0:
```python
import functools
import math

import jax
import jax.numpy as jnp
from jax import lax
from jax.experimental import pallas as pl
from jax.experimental.pallas import tpu as pltpu
from jax.sharding import PartitionSpec as P

BF = jnp.bfloat16
F32 = jnp.float32
ROWS = 24
COLS = 128
CELLS = ROWS * COLS
OFF = 16
WIDE = 160
LO = 8
SPAN = 144
REACH = 136
MESH = pl.DeviceIdType.MESH
N_LAT = 8
N_LON = 16
PIECE = 36
PADDED = 48


def send(src, dst, send_sem, recv_sem, target):
    return pltpu.make_async_remote_copy(
        src_ref=src,
        dst_ref=dst,
        send_sem=send_sem,
        recv_sem=recv_sem,
        device_id=target,
        device_id_type=MESH,
    )


def greet(my_lat, my_lon):
    barrier = pltpu.get_barrier_semaphore()
    peers = [(my_lat, lax.rem(my_lon + d, N_LON)) for d in range(1, N_LON)]
    peers += [(lax.rem(my_lat + d, N_LAT), my_lon) for d in range(1, N_LAT)]
    for down in (1, N_LAT - 1):
        for side in (1, N_LON - 1):
            peers.append((lax.rem(my_lat + down, N_LAT), lax.rem(my_lon + side, N_LON)))
    for peer in peers:
        pl.semaphore_signal(barrier, inc=1, device_id=peer, device_id_type=MESH)
    return barrier, len(peers)


class Sum:
    def __init__(self, my_lat, my_lon, pieces, got, part, parts, whole, sems):
        self.my_lat, self.my_lon = my_lat, my_lon
        self.pieces, self.got, self.part, self.parts, self.whole = pieces, got, part, parts, whole
        self.s1, self.r1, self.s2, self.r2, self.s3, self.r3 = sems

    def lon_peer(self, d):
        return (self.my_lat, lax.rem(self.my_lon + d, N_LON))

    def lat_peer(self, d):
        return (lax.rem(self.my_lat + d, N_LAT), self.my_lon)

    def first(self, d):
        peer = lax.rem(self.my_lon + d, N_LON)
        return send(self.pieces.at[peer], self.got.at[d], self.s1.at[d], self.r1.at[d], self.lon_peer(d))

    def second(self, d):
        return send(self.part, self.parts.at[self.my_lat], self.s2.at[d], self.r2.at[d], self.lat_peer(d))

    def third(self, d):
        mine = self.whole.at[self.my_lon]
        return send(mine, mine, self.s3.at[d], self.r3.at[d], self.lon_peer(d))

    def start_first(self):
        for d in range(1, N_LON):
            self.first(d).start()

    def start_second(self):
        total = self.pieces[self.my_lon].astype(jnp.float32)
        for d in range(1, N_LON):
            self.first(d).wait_recv()
            total = total + self.got[d].astype(jnp.float32)
        rounded = total.astype(jnp.bfloat16)
        self.part[...] = rounded
        self.parts[self.my_lat] = rounded
        for d in range(1, N_LAT):
            self.second(d).start()

    def start_third(self):
        for d in range(1, N_LAT):
            self.second(d).wait_recv()
        total = self.parts[0].astype(jnp.float32)
        for lat in range(1, N_LAT):
            total = total + self.parts[lat].astype(jnp.float32)
        self.whole[self.my_lon] = total.astype(jnp.bfloat16)
        for d in range(1, N_LON):
            self.third(d).start()

    def finish(self, scale, out):
        for d in range(1, N_LON):
            self.third(d).wait_recv()
        for k in range(N_LON):
            piece = self.whole[k].astype(jnp.float32)[:PIECE] * scale
            out[pl.ds(k * PIECE, PIECE), :] = piece
        for d in range(1, N_LON):
            self.first(d).wait_send()
            self.third(d).wait_send()
        for d in range(1, N_LAT):
            self.second(d).wait_send()


class Small(Sum):
    def __init__(self, my_lat, my_lon, mine, got, part, parts, sems):
        self.my_lat, self.my_lon = my_lat, my_lon
        self.mine, self.got, self.part, self.parts = mine, got, part, parts
        self.s1, self.r1, self.s2, self.r2 = sems

    def first(self, d):
        return send(self.mine, self.got.at[d], self.s1.at[d], self.r1.at[d], self.lon_peer(d))

    def start_second(self):
        total = self.mine[...]
        for d in range(1, N_LON):
            self.first(d).wait_recv()
            total = total + self.got[d]
        self.part[...] = total
        for d in range(1, N_LAT):
            self.second(d).start()

    def second(self, d):
        return send(self.part, self.parts.at[d], self.s2.at[d], self.r2.at[d], self.lat_peer(d))

    def finish(self, scale, out):
        total = self.part[...]
        for d in range(1, N_LAT):
            self.second(d).wait_recv()
            total = total + self.parts[d]
        lane = lax.broadcasted_iota(jnp.int32, total.shape, 1)
        mine = lane == self.my_lat * N_LON + self.my_lon
        out[...] = jnp.sum(jnp.where(mine, total, 0.0), axis=1, keepdims=True) * scale
        for d in range(1, N_LON):
            self.first(d).wait_send()
        for d in range(1, N_LAT):
            self.second(d).wait_send()


def sum_scratch():
    return [
        pltpu.VMEM((N_LON, PADDED, 128), jnp.bfloat16),
        pltpu.VMEM((N_LON, PADDED, 128), jnp.bfloat16),
        pltpu.VMEM((PADDED, 128), jnp.bfloat16),
        pltpu.VMEM((N_LAT, PADDED, 128), jnp.bfloat16),
        pltpu.VMEM((N_LON, PADDED, 128), jnp.bfloat16),
    ] + [pltpu.SemaphoreType.DMA((n,)) for n in (N_LON, N_LON, N_LAT, N_LAT, N_LON, N_LON)]


def small_scratch(shape):
    return [
        pltpu.VMEM((N_LON,) + shape, jnp.float32),
        pltpu.VMEM(shape, jnp.float32),
        pltpu.VMEM((N_LAT,) + shape, jnp.float32),
    ] + [pltpu.SemaphoreType.DMA((n,)) for n in (N_LON, N_LON, N_LAT, N_LAT)]


def turned(block):
    eye = (
        lax.broadcasted_iota(jnp.int32, (COLS, COLS), 0)
        == lax.broadcasted_iota(jnp.int32, (COLS, COLS), 1)
    ).astype(BF)
    return lax.dot_general(eye, block, (((1,), (1,)), ((), ())), preferred_element_type=F32)


def row_at(i):
    return pl.ds(pl.multiple_of(i * COLS, COLS), COLS)


def lay_weights(source, target):
    for a in range(3):
        top, mid, end = a * 128, a * 128 + 64, a * 128 + 128
        target[top:mid, 0:128] = source[3 * a + 1]
        target[mid:end, 0:128] = source[3 * a + 2]
        target[top:mid, 128:256] = jnp.zeros((64, 128), BF)
        target[mid:end, 128:256] = source[3 * a]


def loop(low, high, body):
    def step(i, carry):
        body(i)
        return carry

    lax.fori_loop(low, high, step, 0)


def taps_sum(field, row, base, coefs, first, rows_of, cols_of, span):
    acc = field[row, pl.ds(base, span), :]
    for a in range(3):
        for b in range(3):
            coef = coefs[pl.ds(first + 3 * a + b, 1), :]
            acc = acc + coef * field[rows_of(a), pl.ds(cols_of(b), span), :]
    return acc


def kernel(
    scale, x_hbm, c_hbm, cov, wd, wu, kern,
    dec_hbm, gi_hbm, down_out, up_out, small_out,
    xa0, xa1, ma0, ma1, xb0, xb1, mb0, mb1, wdm, wum, yx, ym,
    s0, s1, r2, r1, ds_, d2, pg2, dec, gi, tmp, pack_l, pack_r,
    send_l, send_r, got_l, got_r, got_lc, got_rc, row_x, row_m,
    tile_l, tile_r, e2_up, e2_dn, got_up, got_dn, grad, flat, small_mine,
    in_sem, out_sem, e1_s, e1_r, e2_s, e2_r, e3_s, e3_r, *sums
):
    my_lat, my_lon = lax.axis_index("lat"), lax.axis_index("lon")
    up_lat, dn_lat = lax.rem(my_lat + N_LAT - 1, N_LAT), lax.rem(my_lat + 1, N_LAT)
    lt_lon, rt_lon = lax.rem(my_lon + N_LON - 1, N_LON), lax.rem(my_lon + 1, N_LON)
    has_up = (my_lat > 0).astype(F32)
    has_dn = (my_lat < N_LAT - 1).astype(F32)
    down = Sum(my_lat, my_lon, *sums[:5], sums[5:11])
    up = Sum(my_lat, my_lon, *sums[11:16], sums[16:22])
    small = Small(my_lat, my_lon, small_mine, *sums[22:25], sums[25:29])

    loads = [
        pltpu.make_async_copy(x_hbm.at[0], xa0, in_sem.at[0]),
        pltpu.make_async_copy(x_hbm.at[1], xa1.at[:, pl.ds(COLS, CELLS)], in_sem.at[1]),
        pltpu.make_async_copy(c_hbm.at[0], ma0, in_sem.at[2]),
        pltpu.make_async_copy(c_hbm.at[1], ma1.at[:, pl.ds(COLS, CELLS)], in_sem.at[3]),
    ]
    for load in loads:
        load.start()
    barrier, met = greet(my_lat, my_lon)
    lay_weights(wd, wdm)
    lay_weights(wu, wum)
    spread = (
        lax.broadcasted_iota(jnp.int32, (16, COLS), 0)
        == lax.broadcasted_iota(jnp.int32, (16, COLS), 1) // 8
    ).astype(BF)
    flags = jnp.dot(cov[...].astype(F32).astype(BF), spread, preferred_element_type=F32).astype(BF)
    for load in loads:
        load.wait()

    for q in range(3):
        flag = flags[q : q + 1, :]

        def turn(i, flag=flag):
            here, after = row_at(i), row_at(i + 1)
            ma0[:, here] = ma0[:, here] * flag
            ma1[:, after] = ma1[:, after] * flag
            for u, (field, at, into, shift) in enumerate(
                (
                    (xa0, here, xb0, here),
                    (xa1, after, xb1, after),
                    (ma0, here, mb0, here),
                    (ma1, after, mb1, after),
                )
            ):
                block = turned(field[:, at])
                into[shift, :] = block.astype(BF)
                spot = (u % 2) * 192 + i * 8 + (u // 2) * 4
                pack_l[pl.ds(spot, 4), :] = block[0:4]
                pack_r[pl.ds(spot, 4), :] = block[COLS - 4 : COLS]

        loop(8 * q, 8 * q + 8, turn)
    send_l[...] = pack_l[...].astype(BF)
    send_r[...] = pack_r[...].astype(BF)

    pl.semaphore_wait(barrier, met)
    last = pl.ds(ROWS * COLS, COLS)
    corner = pl.ds(368, 16)
    first = [
        send(send_l, got_r, e1_s.at[0], e1_r.at[0], (my_lat, lt_lon)),
        send(send_r, got_l, e1_s.at[1], e1_r.at[1], (my_lat, rt_lon)),
        send(send_l.at[corner], got_rc, e1_s.at[2], e1_r.at[2], (dn_lat, lt_lon)),
        send(send_r.at[corner], got_lc, e1_s.at[3], e1_r.at[3], (dn_lat, rt_lon)),
        send(xa1.at[:, last], row_x, e1_s.at[4], e1_r.at[4], (dn_lat, my_lon)),
        send(ma1.at[:, last], row_m, e1_s.at[5], e1_r.at[5], (dn_lat, my_lon)),
    ]
    for copy in first:
        copy.start()

    def conv_row(i):
        here, after = row_at(i), row_at(i + 1)
        for b0, b1, weight, y in ((xb0, xb1, wdm, yx), (mb0, mb1, wum, ym)):
            taps = jnp.concatenate([b1[here, :], b0[here, :], b1[after, :]], axis=1)
            y[i, OFF : OFF + COLS, :] = jnp.dot(taps, weight[...], preferred_element_type=F32)

    loop(1, ROWS, conv_row)

    for copy in first:
        copy.wait_recv()
    for got, field, into in ((row_x, xa1, xb1), (row_m, ma1, mb1)):
        row = got[...] * has_up.astype(BF)
        field[:, 0:COLS] = row
        into[0:COLS, :] = turned(row).astype(BF)
    conv_row(0)
    for got, edge, tile, at in ((got_l, got_lc, tile_l, 12), (got_r, got_rc, tile_r, 144)):
        tile[0:8, :] = edge[...].astype(F32)[8:16] * has_up
        tile[8:200, :] = got[192:384, :].astype(F32)
        taps = jnp.concatenate(
            [tile[0:192, :].astype(BF), got[0:192, :], tile[8:200, :].astype(BF)], axis=1
        )
        for weight, y, part in ((wdm, yx, 0), (wum, ym, 4)):
            rim = jnp.dot(taps, weight[...], preferred_element_type=F32)
            for i in range(ROWS):
                y[i, at : at + 4, :] = rim[i * 8 + part : i * 8 + part + 4]

    def activate(i):
        span, before = pl.ds(LO, SPAN), pl.ds(LO - 1, SPAN)
        pre = yx[i, span, 0:128] + yx[i, before, 128:256]
        sig = 0.5 * jnp.tanh(0.5 * pre) + 0.5
        s0[i + 2, span, :] = (pre * sig).astype(BF).astype(F32)
        ds_[i, span, :] = sig * (1.0 + pre * (1.0 - sig))
        grad_row = ym[i, span, 0:128] + ym[i, before, 128:256]
        r2[i + 2, span, :] = grad_row.astype(BF).astype(F32)

    for i in (0, 1, ROWS - 2, ROWS - 1):
        activate(i)
    for n, field in enumerate((s0, r2)):
        for k in range(2):
            at = pl.ds(n * 288 + k * SPAN, SPAN)
            e2_up[at, :] = field[2 + k, LO : LO + SPAN, :].astype(BF)
            e2_dn[at, :] = field[ROWS + k, LO : LO + SPAN, :].astype(BF)
    second = [
        send(e2_up, got_up, e2_s.at[0], e2_r.at[0], (up_lat, my_lon)),
        send(e2_dn, got_dn, e2_s.at[1], e2_r.at[1], (dn_lat, my_lon)),
    ]
    for copy in second:
        copy.start()
    loop(2, ROWS - 2, activate)

    def forward_1(r):
        acc = taps_sum(s0, r + 1, LO, kern, 0, lambda a: r + a, lambda b: LO - 1 + b, SPAN)
        s1[r, pl.ds(LO, SPAN), :] = acc

    def backward_1(r):
        acc = taps_sum(r2, r + 1, LO, kern, 9, lambda a: r - a + 2, lambda b: LO + 1 - b, SPAN)
        r1[r, pl.ds(LO, SPAN), :] = acc

    loop(2, ROWS, forward_1)
    loop(2, ROWS, backward_1)
    for copy in second:
        copy.wait_recv()
    for n, field in enumerate((s0, r2)):
        for k in range(2):
            at = pl.ds(n * 288 + k * SPAN, SPAN)
            field[k, LO : LO + SPAN, :] = got_dn[at, :].astype(F32) * has_up
            field[ROWS + 2 + k, LO : LO + SPAN, :] = got_up[at, :].astype(F32) * has_dn
    for r in (0, 1, ROWS, ROWS + 1):
        forward_1(r)
        backward_1(r)
    for field in (s1, r1):
        field[0, LO : LO + SPAN, :] = field[0, LO : LO + SPAN, :] * has_up
        field[ROWS + 1, LO : LO + SPAN, :] = field[ROWS + 1, LO : LO + SPAN, :] * has_dn

    def pair(value, slot, into, i):
        tmp[slot, 0:REACH, :] = value
        here = row_at(i)
        into[here, 0:128] = tmp[slot, 0:COLS, :].astype(BF)
        into[here, 128:256] = tmp[slot, 1 : COLS + 1, :].astype(BF)

    def backward_0(i):
        acc = taps_sum(r1, i + 1, OFF, kern, 0, lambda a: i - a + 2, lambda b: OFF + 1 - b, REACH)
        value = acc.astype(BF).astype(F32) * ds_[i, pl.ds(OFF, REACH), :]
        pair(value, 0, pg2, i)

    loop(0, ROWS, backward_0)
    third = [
        send(pg2.at[pl.ds(0, COLS)], pg2.at[pl.ds(CELLS, COLS)], e3_s.at[0], e3_r.at[0], (up_lat, my_lon)),
        send(d2.at[pl.ds(0, COLS)], d2.at[pl.ds(CELLS, COLS)], e3_s.at[1], e3_r.at[1], (up_lat, my_lon)),
    ]
    third[0].start()

    def weight_grad(a0, a1, pairs, total):
        grad[...] = jnp.zeros_like(grad)

        def step(n):
            at = pl.ds(pl.multiple_of(n * 512, 512), 512)
            after = pl.ds(pl.multiple_of(n * 512 + COLS, COLS), 512)
            taps = jnp.concatenate([a1[:, at], a0[:, at], a1[:, after]], axis=0)
            grad[...] += jnp.dot(taps, pairs[at, :], preferred_element_type=F32)

        loop(0, ROWS // 4, step)
        for a in range(3):
            top, mid, end = a * 128, a * 128 + 64, a * 128 + 128
            flat[(3 * a + 1) * 64 : (3 * a + 2) * 64, :] = grad[top:mid, 0:128]
            flat[(3 * a + 2) * 64 : (3 * a + 3) * 64, :] = grad[mid:end, 0:128]
            flat[3 * a * 64 : (3 * a + 1) * 64, :] = grad[mid:end, 128:256]
        for k in range(N_LON):
            total.pieces[k] = flat[pl.ds(k * PIECE, PADDED), :].astype(BF)
        total.start_first()

    flat[576:624, :] = jnp.zeros((48, 128), F32)
    weight_grad(xa0, xa1, pg2, down)

    def forward_0(i):
        acc = taps_sum(s1, i + 1, OFF, kern, 9, lambda a: i + a, lambda b: OFF - 1 + b, REACH)
        pair(acc, 1, d2, i)

    loop(0, ROWS, forward_0)
    third[1].start()
    weight_grad(ma0, ma1, d2, up)

    def kernel_grad(left, left_row, right, right_row, first_row):
        def step(i, accs):
            own = left[i + left_row, OFF : OFF + COLS, :]
            found = []
            for a in range(3):
                for b in range(3):
                    other = right[i + a + right_row, pl.ds(OFF - 1 + b, COLS), :]
                    found.append(accs[3 * a + b] + jnp.sum((own * other).reshape(16, 8, 128), axis=0))
            return tuple(found)

        accs = lax.fori_loop(0, ROWS, step, tuple(jnp.zeros((8, 128), F32) for _ in range(9)))
        for t in range(9):
            small_mine[first_row + t : first_row + t + 1, :] = jnp.sum(accs[t], axis=0, keepdims=True)

    small_mine[16:24, :] = jnp.zeros((8, 128), F32)
    kernel_grad(r1, 1, s0, 1, 0)
    kernel_grad(r2, 2, s1, 0, 9)
    small.start_first()

    down.start_second()

    def add_conv(weight, pairs, f0, f1, out):
        def step(n):
            at = pl.ds(pl.multiple_of(n * 512, 512), 512)
            after = pl.ds(pl.multiple_of(n * 512 + COLS, COLS), 512)
            nt = (((1,), (1,)), ((), ()))
            here, below = pairs[at, :], pairs[after, :]
            even = lax.dot_general(weight[128:256, :], here, nt, preferred_element_type=F32)
            odd = lax.dot_general(weight[256:384, :], here, nt, preferred_element_type=F32)
            odd = odd + lax.dot_general(weight[0:128, :], below, nt, preferred_element_type=F32)
            out[0, :, at] = (f0[:, at].astype(F32) + even).astype(BF)
            out[1, :, at] = (f1[:, after].astype(F32) + odd).astype(BF)

        loop(0, ROWS // 4, step)

    below = pl.ds(CELLS, COLS)
    third[1].wait_recv()
    d2[below, :] = d2[below, :] * has_dn.astype(BF)
    add_conv(wum, d2, xa0, xa1, dec)
    store_dec = pltpu.make_async_copy(dec, dec_hbm, out_sem.at[0])
    store_dec.start()
    up.start_second()
    down.start_third()
    small.start_second()
    third[0].wait_recv()
    pg2[below, :] = pg2[below, :] * has_dn.astype(BF)
    add_conv(wdm, pg2, ma0, ma1, gi)
    store_gi = pltpu.make_async_copy(gi, gi_hbm, out_sem.at[1])
    store_gi.start()
    up.start_third()
    down.finish(scale, down_out)
    small.finish(scale, small_out)
    up.finish(scale, up_out)
    for copy in first + second + third:
        copy.wait_send()
    store_dec.wait()
    store_gi.wait()


def level(x, c, cov, wd, wu, kern, scale):
    vmem = pl.BlockSpec(memory_space=pltpu.VMEM)
    hbm = pl.BlockSpec(memory_space=pl.ANY)
    wide = lambda rows: pltpu.VMEM((rows, WIDE, 128), F32)
    mat = lambda rows, cols=128: pltpu.VMEM((rows, cols), BF)
    dma = lambda n: pltpu.SemaphoreType.DMA((n,))
    tall = (ROWS + 1) * COLS
    planes = jax.ShapeDtypeStruct((2, 128, CELLS), BF)
    scratch = (
        [mat(128, CELLS), mat(128, tall)] * 2
        + [mat(CELLS), mat(tall)] * 2
        + [mat(384, 256)] * 2
        + [pltpu.VMEM((ROWS, WIDE, 256), F32)] * 2
        + [wide(ROWS + 4), wide(ROWS + 2), wide(ROWS + 4), wide(ROWS + 2), wide(ROWS)]
        + [mat(tall, 256)] * 2
        + [pltpu.VMEM((2, 128, CELLS), BF)] * 2
        + [pltpu.VMEM((2, REACH, 128), F32)]
        + [pltpu.VMEM((384, 128), F32)] * 2
        + [mat(384)] * 4
        + [mat(16)] * 2
        + [mat(128)] * 2
        + [pltpu.VMEM((200, 128), F32)] * 2
        + [mat(576)] * 4
        + [pltpu.VMEM((384, 256), F32), pltpu.VMEM((624, 128), F32), pltpu.VMEM((24, 128), F32)]
        + [dma(4), dma(2), dma(6), dma(6), dma(2), dma(2), dma(2), dma(2)]
        + sum_scratch()
        + sum_scratch()
        + small_scratch((24, 128))
    )
    return pl.pallas_call(
        functools.partial(kernel, scale),
        out_shape=(
            planes,
            planes,
            jax.ShapeDtypeStruct((576, 128), F32),
            jax.ShapeDtypeStruct((576, 128), F32),
            jax.ShapeDtypeStruct((24, 1), F32),
        ),
        in_specs=[hbm, hbm, vmem, vmem, vmem, vmem],
        out_specs=(hbm, hbm, vmem, vmem, vmem),
        scratch_shapes=scratch,
        compiler_params=pltpu.CompilerParams(
            collective_id=0, has_side_effects=True, vmem_limit_bytes=56 * 1024 * 1024
        ),
        cost_estimate=pl.CostEstimate(flops=3_600_000_000, bytes_accessed=7_000_000, transcendentals=500_000),
    )(x, c, cov, wd, wu, kern)


def shards(inputs, kernels, w_down, w_up, cotangent, coverage):
    total = inputs.shape[3] * inputs.shape[4] * N_LAT * N_LON
    scale = 1.0 / math.sqrt(total)

    def gathered(planes):
        return jnp.transpose(planes, (1, 2, 0, 3, 4)).reshape(2, 128, CELLS)

    def spread(planes):
        return jnp.transpose(planes.reshape(2, 2, 64, ROWS, COLS), (2, 0, 1, 3, 4))

    decoded, grad_input, down, up, small = level(
        gathered(inputs),
        gathered(cotangent),
        coverage,
        jnp.transpose(w_down, (0, 2, 1)),
        w_up,
        kernels.reshape(18, 128),
        scale,
    )
    return (
        spread(decoded),
        spread(grad_input),
        jnp.transpose(down.reshape(9, 64, 128), (0, 2, 1)),
        up.reshape(9, 64, 128),
        small[:18].reshape(2, 9, 1),
    )


def solution(mesh):
    placed = (
        P(None, None, None, "lat", "lon"),
        P(),
        P(),
        P(),
        P(None, None, None, "lat", "lon"),
        P("lat", "lon"),
    )
    return jax.shard_map(
        shards,
        mesh=mesh,
        in_specs=placed,
        out_specs=(
            P(None, None, None, "lat", "lon"),
            P(None, None, None, "lat", "lon"),
            P(),
            P(),
            P(None, None, ("lat", "lon")),
        ),
        check_vma=False,
    )
```

profile of v0, /device:TPU:1, one launch (start us, length us, event | category | flops | bytes accessed | tf_op | source)
XLA Modules:
  0.0 64.4 jit_solution(16561434029919779624)
XLA Ops:
  0.6 0.7 %copy.19 = f32[2,9,128]{2,1,0:T(8,128)S(1)} copy(f32[2,9,128]{2,0,1:T(2,128)} %param.7) | data formatting | bytes 18432 | tf_op args[1]
  1.3 0.6 reshape.36.kern
  1.9 1.7 %copy.17 = bf16[2,2,64,24,128]{4,3,2,1,0:T(8,128)(2,1)S(1)} copy(bf16[2,2,64,24,128]{4,3,1,0,2:T(8,128)(2,1)} %bitcast.26) | data formatting | bytes 3145728 | tf_op jit(solution)/shard_map/transpose | solution.py:513
  3.6 0.0 copy-start
  3.6 1.6 %reshape.34.x_hbm = bf16[2,128,3072]{2,1,0:T(8,128)(2,1)} reshape(bf16[2,2,64,24,128]{4,3,2,1,0:T(8,128)(2,1)S(1)} %copy.17) | data formatting | bytes 3145728 | tf_op jit(solution)/shard_map/reshape | solution.py:513
  5.2 0.1 copy-done
  5.3 0.3 copy.18
  5.5 1.6 %reshape.35.c_hbm = bf16[2,128,3072]{2,1,0:T(8,128)(2,1)} reshape(bf16[2,2,64,24,128]{4,3,2,1,0:T(8,128)(2,1)S(1)} %copy.18) | data formatting | bytes 3145728 | tf_op jit(solution)/shard_map/reshape | solution.py:513
  7.1 50.7 %shard_map.101 = (bf16[2,128,3072]{2,1,0:T(8,128)(2,1)}, bf16[2,128,3072]{2,1,0:T(8,128)(2,1)}, f32[576,128]{1,0:T(8,128)}, f32[576,128]{1,0:T(8,128)}, f32[24,1]{1,0:T(8,128)}) custom-call(bf16[2,128,3072]{2,1,0:T(8,128)(2,1)} %reshape.34.x_hbm, bf16[2,128,3072]{2,1,0:T(8,128)(2,1)} %reshape.35.c_hbm, s32[3,16]{1,0:T(4,128)} %cov.1, ...), custom_call_target="tpu_custom_call" | custom-call | flops 3600000000 | bytes 7000000 | tf_op jit(solution)/shard_map/pallas_call | solution.py:489
  57.8 0.0 copy-start.1
  57.8 1.8 %copy.23 = bf16[32,8,24,128]{3,2,1,0:T(8,128)(2,1)S(1)} copy(bf16[32,8,24,128]{3,1,2,0:T(8,128)(2,1)} %bitcast.29) | data formatting | bytes 3145728
  59.6 0.0 copy-done.1
  59.7 0.3 copy.24
  60.0 0.0 copy-start.4
  60.0 0.0 copy-start.3
  60.0 0.0 copy-start.2
  60.0 2.2 %copy_bitcast_fusion = (bf16[64,2,2,24,128]{4,3,2,1,0:T(8,128)(2,1)}, bf16[64,2,2,24,128]{4,3,2,1,0:T(8,128)(2,1)}) fusion(bf16[2,2,64,24,128]{4,3,2,1,0:T(8,128)(2,1)S(1)} %bitcast.25, bf16[2,2,64,24,128]{4,3,2,1,0:T(8,128)(2,1)S(1)} %bitcast.24), kind=kLoop, calls=%fused_computation | loop fusion | bytes 6291456 | tf_op jit(solution)/shard_map/transpose | solution.py:516
  62.2 0.0 copy-done.4
  62.2 0.1 slice_reduce_fusion
  62.3 0.7 %reshape.41 = f32[2,9,1]{1,0,2:T(2,128)} reshape(f32[18]{0:T(128)S(1)} %slice_reduce_fusion) | data formatting | bytes 144 | tf_op jit(solution)/shard_map/reshape | solution.py:532
  63.0 0.0 copy-done.3
  63.0 0.7 %copy.29 = f32[9,128,64]{1,2,0:T(8,128)} copy(f32[9,128,64]{1,2,0:T(8,128)S(1)} %bitcast.31) | data formatting | bytes 589824
  63.7 0.0 copy-done.2
  63.7 0.7 %copy.30 = f32[9,64,128]{2,1,0:T(8,128)} copy(f32[9,64,128]{2,1,0:T(8,128)S(1)} %bitcast.30) | data formatting | bytes 589824
Async XLA Ops:
  3.6 1.6 %copy-start = (bf16[64,2,2,24,128]{4,3,2,1,0:T(8,128)(2,1)S(1)}, bf16[64,2,2,24,128]{4,3,2,1,0:T(8,128)(2,1)}, u32[]{:S(2)}) copy-start(bf16[64,2,2,24,128]{4,3,2,1,0:T(8,128)(2,1)} %param.10) | copy-start | bytes 4718596
  57.8 1.9 %copy-start.1 = (bf16[2,128,3072]{2,1,0:T(8,128)(2,1)S(1)}, bf16[2,128,3072]{2,1,0:T(8,128)(2,1)}, u32[]{:S(2)}) copy-start(bf16[2,128,3072]{2,1,0:T(8,128)(2,1)} %get-tuple-element.11) | copy-start | bytes 4718596
  60.0 2.2 %copy-start.4 = (f32[24,1]{1,0:T(8,128)S(1)}, f32[24,1]{1,0:T(8,128)}, u32[]{:S(2)}) copy-start(f32[24,1]{1,0:T(8,128)} %get-tuple-element.14) | copy-start | bytes 292
  60.0 3.0 %copy-start.3 = (f32[576,128]{1,0:T(8,128)S(1)}, f32[576,128]{1,0:T(8,128)}, u32[]{:S(2)}) copy-start(f32[576,128]{1,0:T(8,128)} %get-tuple-element.12) | copy-start | bytes 884740
  60.0 3.7 %copy-start.2 = (f32[576,128]{1,0:T(8,128)S(1)}, f32[576,128]{1,0:T(8,128)}, u32[]{:S(2)}) copy-start(f32[576,128]{1,0:T(8,128)} %get-tuple-element.13) | copy-start | bytes 884740
where the time goes:
time: 64.7 us; the launch traced here: 64.4 us
  Pallas kernels  50.7 us (78%)
  local copies, waits for them, and re-layouts  13 us (20%)
  between operations  0.71 us (1%)
    pallas_call x1, Pallas kernels, level(): pl.pallas_call(functools.partial(kernel, scale), out_shape=(planes, plane...  50.7 us
    unnamed x15, local copies, waits for them, and re-layouts  4.38 us
    reshape x2, local copies, waits for them, and re-layouts, gathered(): return jnp.transpose(planes, (1, 2, 0, 3, 4)).reshape(2, 128, CELLS)  3.16 us
    transpose x1, local copies, waits for them, and re-layouts, spread(): return jnp.transpose(planes.reshape(2, 2, 64, ROWS, COLS), (2, 0, 1, 3, 4))  2.2 us
    transpose x2, local copies, waits for them, and re-layouts, gathered(): return jnp.transpose(planes, (1, 2, 0, 3, 4)).reshape(2, 128, CELLS)  1.95 us

commit v1 on v0

v1 whole, which is shorter than its diff:
```python
import functools
import math

import jax
import jax.numpy as jnp
from jax import lax
from jax.experimental import pallas as pl
from jax.experimental.pallas import tpu as pltpu
from jax.sharding import PartitionSpec as P

BF = jnp.bfloat16
F32 = jnp.float32
ROWS = 24
COLS = 128
CELLS = ROWS * COLS
OFF = 16
WIDE = 160
LO = 8
SPAN = 144
REACH = 136
MESH = pl.DeviceIdType.MESH
N_LAT = 8
N_LON = 16
PIECE = 36
PADDED = 48


def send(src, dst, send_sem, recv_sem, target):
    return pltpu.make_async_remote_copy(
        src_ref=src,
        dst_ref=dst,
        send_sem=send_sem,
        recv_sem=recv_sem,
        device_id=target,
        device_id_type=MESH,
    )


def greet(my_lat, my_lon):
    barrier = pltpu.get_barrier_semaphore()
    peers = [(my_lat, lax.rem(my_lon + d, N_LON)) for d in range(1, N_LON)]
    peers += [(lax.rem(my_lat + d, N_LAT), my_lon) for d in range(1, N_LAT)]
    for down in (1, N_LAT - 1):
        for side in (1, N_LON - 1):
            peers.append((lax.rem(my_lat + down, N_LAT), lax.rem(my_lon + side, N_LON)))
    for peer in peers:
        pl.semaphore_signal(barrier, inc=1, device_id=peer, device_id_type=MESH)
    return barrier, len(peers)


class Sum:
    def __init__(self, my_lat, my_lon, pieces, got, part, parts, whole, *sems):
        self.my_lat, self.my_lon = my_lat, my_lon
        self.pieces, self.got, self.part, self.parts, self.whole = pieces, got, part, parts, whole
        self.s1, self.r1, self.s2, self.r2, self.s3, self.r3 = sems

    def lon_peer(self, d):
        return (self.my_lat, lax.rem(self.my_lon + d, N_LON))

    def lat_peer(self, d):
        return (lax.rem(self.my_lat + d, N_LAT), self.my_lon)

    def first(self, d):
        peer = lax.rem(self.my_lon + d, N_LON)
        return send(self.pieces.at[peer], self.got.at[d], self.s1, self.r1, self.lon_peer(d))

    def second(self, d):
        return send(self.part, self.parts.at[d], self.s2, self.r2, self.lat_peer(d))

    def third(self, d):
        return send(self.part, self.whole.at[d], self.s3, self.r3, self.lon_peer(d))

    def all_of(self, buffer, sent, received):
        arrived = buffer.at[pl.ds(1, buffer.shape[0] - 1)]
        return send(arrived, arrived, sent, received, self.lon_peer(1))

    def start_first(self):
        for d in range(1, N_LON):
            self.first(d).start()

    def start_second(self):
        self.all_of(self.got, self.s1, self.r1).wait_recv()
        total = self.pieces[self.my_lon].astype(jnp.float32)
        for d in range(1, N_LON):
            total = total + self.got[d].astype(jnp.float32)
        rounded = total.astype(jnp.bfloat16)
        self.part[...] = rounded
        self.parts[0] = rounded
        for d in range(1, N_LAT):
            self.second(d).start()

    def start_third(self):
        self.all_of(self.parts, self.s2, self.r2).wait()
        total = jnp.zeros((PADDED, 128), jnp.float32)
        for lat in range(N_LAT):
            slot = lax.rem(self.my_lat - lat + N_LAT, N_LAT)
            total = total + self.parts[slot].astype(jnp.float32)
        rounded = total.astype(jnp.bfloat16)
        self.part[...] = rounded
        self.whole[0] = rounded
        for d in range(1, N_LON):
            self.third(d).start()

    def finish(self, scale, out):
        self.all_of(self.whole, self.s3, self.r3).wait_recv()
        for d in range(N_LON):
            k = lax.rem(self.my_lon - d + N_LON, N_LON)
            piece = self.whole[d].astype(jnp.float32)[:PIECE] * scale
            out[pl.ds(k * PIECE, PIECE), :] = piece

    def settle(self):
        self.all_of(self.got, self.s1, self.r1).wait_send()
        self.all_of(self.whole, self.s3, self.r3).wait_send()


class Small(Sum):
    def __init__(self, my_lat, my_lon, mine, got, part, parts, *sems):
        self.my_lat, self.my_lon = my_lat, my_lon
        self.mine, self.got, self.part, self.parts = mine, got, part, parts
        self.s1, self.r1, self.s2, self.r2 = sems

    def first(self, d):
        return send(self.mine, self.got.at[d], self.s1, self.r1, self.lon_peer(d))

    def start_second(self):
        self.all_of(self.got, self.s1, self.r1).wait_recv()
        total = self.mine[...]
        for d in range(1, N_LON):
            total = total + self.got[d]
        self.part[...] = total
        for d in range(1, N_LAT):
            self.second(d).start()

    def finish(self, scale, out):
        self.all_of(self.parts, self.s2, self.r2).wait_recv()
        total = self.part[...]
        for d in range(1, N_LAT):
            total = total + self.parts[d]
        lane = lax.broadcasted_iota(jnp.int32, total.shape, 1)
        mine = lane == self.my_lat * N_LON + self.my_lon
        column = jnp.sum(jnp.where(mine, total, 0.0), axis=1, keepdims=True) * scale
        row = lax.broadcasted_iota(jnp.int32, total.shape, 0)
        for t in range(2):
            line = jnp.sum(jnp.where(row == lane + 9 * t, column, 0.0), axis=0, keepdims=True)
            out[t] = line[:, 0:9]

    def settle(self):
        self.all_of(self.got, self.s1, self.r1).wait_send()
        self.all_of(self.parts, self.s2, self.r2).wait_send()


def sum_scratch():
    return [
        pltpu.VMEM((N_LON, PADDED, 128), jnp.bfloat16),
        pltpu.VMEM((N_LON, PADDED, 128), jnp.bfloat16),
        pltpu.VMEM((PADDED, 128), jnp.bfloat16),
        pltpu.VMEM((N_LAT, PADDED, 128), jnp.bfloat16),
        pltpu.VMEM((N_LON, PADDED, 128), jnp.bfloat16),
    ] + [pltpu.SemaphoreType.DMA] * 6


def small_scratch(shape):
    return [
        pltpu.VMEM((N_LON,) + shape, jnp.float32),
        pltpu.VMEM(shape, jnp.float32),
        pltpu.VMEM((N_LAT,) + shape, jnp.float32),
    ] + [pltpu.SemaphoreType.DMA] * 4


def row_at(i):
    return pl.ds(pl.multiple_of(i * COLS, COLS), COLS)


def lay_weights(source, target):
    for a in range(3):
        top, mid, end = a * 128, a * 128 + 64, a * 128 + 128
        target[top:mid, 0:128] = source[3 * a + 1]
        target[mid:end, 0:128] = source[3 * a + 2]
        target[top:mid, 128:256] = jnp.zeros((64, 128), BF)
        target[mid:end, 128:256] = source[3 * a]


def loop(low, high, body, wide=1):
    def step(n, carry):
        for k in range(wide):
            body(low + n * wide + k)
        return carry

    lax.fori_loop(0, (high - low) // wide, step, 0)


def plane_rows(i):
    return pl.ds(i, 64, stride=ROWS)


def taps_sum(field, row, base, coefs, first, rows_of, cols_of, span):
    acc = field[row, pl.ds(base, span), :]
    for a in range(3):
        for b in range(3):
            coef = coefs[3 * a + b, first : first + 1, :]
            acc = acc + coef * field[rows_of(a), pl.ds(cols_of(b), span), :]
    return acc


def kernel(
    scale, x_hbm, c_hbm, cov_hbm, wd_hbm, wu_hbm, kern_hbm,
    dec_hbm, gi_hbm, down_hbm, up_hbm, small_hbm,
    xa0, xa1, ma0, ma1, xb0, xb1, mb0, mb1, wdm, wum, yx, ym,
    s0, s1, r2, r1, ds_, d2, pg2, tmp, pack_l, pack_r,
    down_out, up_out, small_out, cov, wd, wu, kern, raw_x, raw_c, planes_x, planes_c, send_l, send_r, got_l, got_r, got_lc, got_rc, row_x, row_m,
    tile_l, tile_r, e2_up, e2_dn, got_up, got_dn, grad, flat, small_mine,
    in_sem, out_sem, e1_s, e1_r, e2_s, e2_r, e3_s, e3_r, *sums
):
    my_lat, my_lon = lax.axis_index("lat"), lax.axis_index("lon")
    up_lat, dn_lat = lax.rem(my_lat + N_LAT - 1, N_LAT), lax.rem(my_lat + 1, N_LAT)
    lt_lon, rt_lon = lax.rem(my_lon + N_LON - 1, N_LON), lax.rem(my_lon + 1, N_LON)
    has_up = (my_lat > 0).astype(F32)
    has_dn = (my_lat < N_LAT - 1).astype(F32)
    down = Sum(my_lat, my_lon, *sums[:11])
    up = Sum(my_lat, my_lon, *sums[11:22])
    small = Small(my_lat, my_lon, small_mine, *sums[22:29])

    loads = []
    for n, (source, raw) in enumerate(((x_hbm, raw_x), (c_hbm, raw_c))):
        for u in range(2):
            for v in range(2):
                p = 2 * u + v
                loads.append(
                    pltpu.make_async_copy(source.at[:, u, v], raw.at[p], in_sem.at[4 * n + p])
                )
    params = [
        pltpu.make_async_copy(source, target, in_sem.at[8 + n])
        for n, (source, target) in enumerate(
            ((cov_hbm, cov), (wd_hbm, wd), (wu_hbm, wu), (kern_hbm, kern))
        )
    ]
    for load in params + loads:
        load.start()
    barrier, met = greet(my_lat, my_lon)
    for load in params:
        load.wait()
    lay_weights(wd, wdm)
    lay_weights(wu, wum)
    spread = (
        lax.broadcasted_iota(jnp.int32, (16, COLS), 0)
        == lax.broadcasted_iota(jnp.int32, (16, COLS), 1) // 8
    ).astype(BF)
    flags = jnp.dot(cov[...].astype(F32).astype(BF), spread, preferred_element_type=F32).astype(BF)

    def unfold(raw, planes, p):
        def step(g):
            block = raw[p, pl.ds(g * 16, 16)].astype(F32)
            planes[p, pl.ds(pl.multiple_of(g * 384, 384), 384), :] = block.reshape(384, COLS)

        loop(0, 4, step)

    def turn(u, flag, planes, field, into, part, i):
        at = row_at(i + u)
        block = jnp.concatenate(
            [planes[2 * u, plane_rows(i), :], planes[2 * u + 1, plane_rows(i), :]], axis=0
        ).astype(BF)
        if flag is not None:
            block = block * flag
        field[:, at] = block
        block = block.T
        into[at, :] = block
        block = block.astype(F32)
        spot = u * 192 + i * 8 + part
        pack_l[pl.ds(spot, 4), :] = block[0:4]
        pack_r[pl.ds(spot, 4), :] = block[COLS - 4 : COLS]

    for u, field, into in ((0, xa0, xb0), (1, xa1, xb1)):
        for v in range(2):
            loads[2 * u + v].wait()
            unfold(raw_x, planes_x, 2 * u + v)
        loop(0, ROWS, functools.partial(turn, u, None, planes_x, field, into, 0), 4)
    for u, field, into in ((0, ma0, mb0), (1, ma1, mb1)):
        for v in range(2):
            loads[4 + 2 * u + v].wait()
            unfold(raw_c, planes_c, 2 * u + v)
        for q in range(3):
            body = functools.partial(turn, u, flags[q : q + 1, :], planes_c, field, into, 4)
            loop(8 * q, 8 * q + 8, body, 4)
    send_l[...] = pack_l[...].astype(BF)
    send_r[...] = pack_r[...].astype(BF)

    pl.semaphore_wait(barrier, met)
    last = pl.ds(ROWS * COLS, COLS)
    corner = pl.ds(368, 16)
    first = [
        send(send_l, got_r, e1_s.at[0], e1_r.at[0], (my_lat, lt_lon)),
        send(send_r, got_l, e1_s.at[1], e1_r.at[1], (my_lat, rt_lon)),
        send(send_l.at[corner], got_rc, e1_s.at[2], e1_r.at[2], (dn_lat, lt_lon)),
        send(send_r.at[corner], got_lc, e1_s.at[3], e1_r.at[3], (dn_lat, rt_lon)),
        send(xa1.at[:, last], row_x, e1_s.at[4], e1_r.at[4], (dn_lat, my_lon)),
        send(ma1.at[:, last], row_m, e1_s.at[5], e1_r.at[5], (dn_lat, my_lon)),
    ]
    for copy in first:
        copy.start()

    def conv_rows(i, count):
        here = pl.ds(pl.multiple_of(i * COLS, COLS), count * COLS)
        after = pl.ds(pl.multiple_of((i + 1) * COLS, COLS), count * COLS)
        for b0, b1, weight, y in ((xb0, xb1, wdm, yx), (mb0, mb1, wum, ym)):
            taps = jnp.concatenate([b1[here, :], b0[here, :], b1[after, :]], axis=1)
            found = jnp.dot(taps, weight[...], preferred_element_type=F32)
            for k in range(count):
                y[i + k, OFF : OFF + COLS, :] = found[k * COLS : (k + 1) * COLS]

    conv_rows(1, 3)
    loop(1, ROWS // 4, lambda n: conv_rows(4 * n, 4))

    def activate(i, low=LO, count=SPAN):
        span, before = pl.ds(low, count), pl.ds(low - 1, count)
        pre = yx[i, span, 0:128] + yx[i, before, 128:256]
        sig = 0.5 * jnp.tanh(0.5 * pre) + 0.5
        s0[i + 2, span, :] = (pre * sig).astype(BF).astype(F32)
        ds_[i, span, :] = sig * (1.0 + pre * (1.0 - sig))
        grad_row = ym[i, span, 0:128] + ym[i, before, 128:256]
        r2[i + 2, span, :] = grad_row.astype(BF).astype(F32)

    def rims(i):
        activate(i, LO, 16)
        activate(i, OFF + COLS, 8)

    loop(1, ROWS - 1, activate, 2)
    activate(ROWS - 1)

    for copy in first:
        copy.wait_recv()
    for got, field, into in ((row_x, xa1, xb1), (row_m, ma1, mb1)):
        row = got[...] * has_up.astype(BF)
        field[:, 0:COLS] = row
        into[0:COLS, :] = row.T
    conv_rows(0, 1)
    for got, edge, tile, at in ((got_l, got_lc, tile_l, 12), (got_r, got_rc, tile_r, 144)):
        tile[0:8, :] = edge[...].astype(F32)[8:16] * has_up
        tile[8:200, :] = got[192:384, :].astype(F32)
        taps = jnp.concatenate(
            [tile[0:192, :].astype(BF), got[0:192, :], tile[8:200, :].astype(BF)], axis=1
        )
        for weight, y, part in ((wdm, yx, 0), (wum, ym, 4)):
            rim = jnp.dot(taps, weight[...], preferred_element_type=F32)
            for i in range(ROWS):
                y[i, at : at + 4, :] = rim[i * 8 + part : i * 8 + part + 4]

    for i in (0, 1, ROWS - 2, ROWS - 1):
        rims(i) if i else activate(i)
    for n, field in enumerate((s0, r2)):
        for k in range(2):
            at = pl.ds(n * 288 + k * SPAN, SPAN)
            e2_up[at, :] = field[2 + k, LO : LO + SPAN, :].astype(BF)
            e2_dn[at, :] = field[ROWS + k, LO : LO + SPAN, :].astype(BF)
    second = [
        send(e2_up, got_up, e2_s.at[0], e2_r.at[0], (up_lat, my_lon)),
        send(e2_dn, got_dn, e2_s.at[1], e2_r.at[1], (dn_lat, my_lon)),
    ]
    for copy in second:
        copy.start()
    loop(2, ROWS - 2, rims, 4)

    def forward_1(r):
        acc = taps_sum(s0, r + 1, LO, kern, 0, lambda a: r + a, lambda b: LO - 1 + b, SPAN)
        s1[r, pl.ds(LO, SPAN), :] = acc

    def backward_1(r):
        acc = taps_sum(r2, r + 1, LO, kern, 1, lambda a: r - a + 2, lambda b: LO + 1 - b, SPAN)
        r1[r, pl.ds(LO, SPAN), :] = acc

    loop(2, ROWS, forward_1, 2)
    loop(2, ROWS, backward_1, 2)
    def pair(value, slot, into, i):
        slot = slot + lax.rem(i, 2)
        tmp[slot, 0:REACH, :] = value
        here = row_at(i)
        into[here, 0:128] = tmp[slot, 0:COLS, :].astype(BF)
        into[here, 128:256] = tmp[slot, 1 : COLS + 1, :].astype(BF)

    def backward_0(i):
        acc = taps_sum(r1, i + 1, OFF, kern, 0, lambda a: i - a + 2, lambda b: OFF + 1 - b, REACH)
        value = acc.astype(BF).astype(F32) * ds_[i, pl.ds(OFF, REACH), :]
        pair(value, 0, pg2, i)

    def forward_0(i):
        acc = taps_sum(s1, i + 1, OFF, kern, 1, lambda a: i + a, lambda b: OFF - 1 + b, REACH)
        pair(acc, 2, d2, i)

    loop(2, ROWS - 2, backward_0, 2)
    loop(2, ROWS - 2, forward_0, 2)
    for copy in second:
        copy.wait_recv()
    for n, field in enumerate((s0, r2)):
        for k in range(2):
            at = pl.ds(n * 288 + k * SPAN, SPAN)
            field[k, LO : LO + SPAN, :] = got_dn[at, :].astype(F32) * has_up
            field[ROWS + 2 + k, LO : LO + SPAN, :] = got_up[at, :].astype(F32) * has_dn
    for r in (0, 1, ROWS, ROWS + 1):
        forward_1(r)
        backward_1(r)
    for field in (s1, r1):
        field[0, LO : LO + SPAN, :] = field[0, LO : LO + SPAN, :] * has_up
        field[ROWS + 1, LO : LO + SPAN, :] = field[ROWS + 1, LO : LO + SPAN, :] * has_dn

    for i in (0, 1, ROWS - 2, ROWS - 1):
        backward_0(i)
        forward_0(i)
    third = [
        send(pg2.at[pl.ds(0, COLS)], pg2.at[pl.ds(CELLS, COLS)], e3_s.at[0], e3_r.at[0], (up_lat, my_lon)),
        send(d2.at[pl.ds(0, COLS)], d2.at[pl.ds(CELLS, COLS)], e3_s.at[1], e3_r.at[1], (up_lat, my_lon)),
    ]
    for copy in third:
        copy.start()

    def weight_grad(a0, a1, pairs, total):
        half = CELLS // 2
        for n in range(2):
            at, after = pl.ds(n * half, half), pl.ds(n * half + COLS, half)
            taps = jnp.concatenate([a1[:, at], a0[:, at], a1[:, after]], axis=0)
            part = jnp.dot(taps, pairs[at, :], preferred_element_type=F32)
            grad[...] = part if n == 0 else grad[...] + part
        for a in range(3):
            top, mid, end = a * 128, a * 128 + 64, a * 128 + 128
            flat[(3 * a + 1) * 64 : (3 * a + 2) * 64, :] = grad[top:mid, 0:128]
            flat[(3 * a + 2) * 64 : (3 * a + 3) * 64, :] = grad[mid:end, 0:128]
            flat[3 * a * 64 : (3 * a + 1) * 64, :] = grad[mid:end, 128:256]
        for k in range(N_LON):
            total.pieces[k] = flat[pl.ds(k * PIECE, PADDED), :].astype(BF)
        total.start_first()

    flat[576:624, :] = jnp.zeros((48, 128), F32)
    weight_grad(xa0, xa1, pg2, down)

    weight_grad(ma0, ma1, d2, up)

    def kernel_grad(left, left_row, right, right_row, first_row):
        def step(i, accs):
            own = left[i + left_row, OFF : OFF + COLS, :]
            found = []
            for a in range(3):
                for b in range(3):
                    other = right[i + a + right_row, pl.ds(OFF - 1 + b, COLS), :]
                    found.append(accs[3 * a + b] + jnp.sum((own * other).reshape(16, 8, 128), axis=0))
            return tuple(found)

        accs = lax.fori_loop(0, ROWS, step, tuple(jnp.zeros((8, 128), F32) for _ in range(9)))
        for t in range(9):
            small_mine[first_row + t : first_row + t + 1, :] = jnp.sum(accs[t], axis=0, keepdims=True)

    small_mine[16:24, :] = jnp.zeros((8, 128), F32)
    kernel_grad(r1, 1, s0, 1, 0)
    kernel_grad(r2, 2, s1, 0, 9)
    small.start_first()

    def add_piece(weight, pairs, f0, f1, planes, n):
        at = pl.ds(pl.multiple_of(n * 512, 512), 512)
        after = pl.ds(pl.multiple_of(n * 512 + COLS, COLS), 512)
        lines = jnp.concatenate([pairs[row_at(4 * n + k), :].T for k in range(5)], axis=1)
        found = jnp.dot(weight[128:384, :], lines[:, 0:512], preferred_element_type=F32)
        under = jnp.dot(weight[0:128, :], lines[:, COLS:640], preferred_element_type=F32)
        even = f0[:, at].astype(F32) + found[0:128]
        odd = f1[:, after].astype(F32) + found[128:256] + under
        for u, value in ((0, even), (1, odd)):
            for k in range(4):
                for v in range(2):
                    planes[2 * u + v, plane_rows(4 * n + k), :] = value[
                        v * 64 : (v + 1) * 64, k * COLS : (k + 1) * COLS
                    ]

    def put_out(planes, raw, out, sem):
        stores = []
        for u in range(2):
            for v in range(2):
                p = 2 * u + v

                def fold(g, p=p):
                    block = planes[p, pl.ds(pl.multiple_of(g * 384, 384), 384), :]
                    raw[p, pl.ds(g * 16, 16)] = block.astype(BF).reshape(16, ROWS, COLS)

                loop(0, 4, fold)
                stores.append(pltpu.make_async_copy(raw.at[p], out.at[:, u, v], sem.at[p]))
                stores[-1].start()
        return stores

    dec_piece = functools.partial(add_piece, wum, d2, xa0, xa1, planes_x)
    gi_piece = functools.partial(add_piece, wdm, pg2, ma0, ma1, planes_c)
    below = pl.ds(CELLS, COLS)

    loop(0, 3, dec_piece)
    down.start_second()
    for copy, field in zip(third, (pg2, d2)):
        copy.wait_recv()
        field[below, :] = field[below, :] * has_dn.astype(BF)
    loop(3, 6, dec_piece)
    stores = put_out(planes_x, raw_x, dec_hbm, out_sem)
    up.start_second()
    loop(0, 2, gi_piece)
    down.start_third()
    small.start_second()
    loop(2, 4, gi_piece)
    up.start_third()
    loop(4, 6, gi_piece)
    stores += put_out(planes_c, raw_c, gi_hbm, out_sem.at[pl.ds(4, 4)])
    down.finish(scale, down_out)
    stores.append(pltpu.make_async_copy(down_out, down_hbm, out_sem.at[8]))
    stores[-1].start()
    small.finish(scale, small_out)
    stores.append(pltpu.make_async_copy(small_out, small_hbm, out_sem.at[9]))
    stores[-1].start()
    up.finish(scale, up_out)
    stores.append(pltpu.make_async_copy(up_out, up_hbm, out_sem.at[10]))
    stores[-1].start()
    for copy in first + second + third:
        copy.wait_send()
    for each in (down, up, small):
        each.settle()
    for store in stores:
        store.wait()


def level(x, c, cov, wd, wu, kern, scale):
    hbm = pl.BlockSpec(memory_space=pl.ANY)
    wide = lambda rows: pltpu.VMEM((rows, WIDE, 128), F32)
    mat = lambda rows, cols=128: pltpu.VMEM((rows, cols), BF)
    dma = lambda n: pltpu.SemaphoreType.DMA((n,))
    tall = (ROWS + 1) * COLS
    planes = jax.ShapeDtypeStruct((64, 2, 2, ROWS, COLS), BF)
    scratch = (
        [mat(128, CELLS), mat(128, tall)] * 2
        + [mat(CELLS), mat(tall)] * 2
        + [mat(384, 256)] * 2
        + [pltpu.VMEM((ROWS, WIDE, 256), F32)] * 2
        + [wide(ROWS + 4), wide(ROWS + 2), wide(ROWS + 4), wide(ROWS + 2), wide(ROWS)]
        + [mat(tall, 256)] * 2
        + [pltpu.VMEM((4, REACH, 128), F32)]
        + [pltpu.VMEM((384, 128), F32)] * 2
        + [pltpu.VMEM((576, 128), F32)] * 2
        + [pltpu.VMEM((2, 1, 9), F32)]
        + [pltpu.VMEM((3, 16), jnp.int32), pltpu.VMEM((9, 64, 128), BF), pltpu.VMEM((9, 64, 128), BF)]
        + [pltpu.VMEM((9, 2, 128), F32)]
        + [pltpu.VMEM((4, 64, ROWS, COLS), BF)] * 2
        + [pltpu.VMEM((4, 64 * ROWS, COLS), F32)] * 2
        + [mat(384)] * 4
        + [mat(16)] * 2
        + [mat(128)] * 2
        + [pltpu.VMEM((200, 128), F32)] * 2
        + [mat(576)] * 4
        + [pltpu.VMEM((384, 256), F32), pltpu.VMEM((624, 128), F32), pltpu.VMEM((24, 128), F32)]
        + [dma(12), dma(11), dma(6), dma(6), dma(2), dma(2), dma(2), dma(2)]
        + sum_scratch()
        + sum_scratch()
        + small_scratch((24, 128))
    )
    return pl.pallas_call(
        functools.partial(kernel, scale),
        out_shape=(
            planes,
            planes,
            jax.ShapeDtypeStruct((576, 128), F32),
            jax.ShapeDtypeStruct((576, 128), F32),
            jax.ShapeDtypeStruct((2, 1, 9), F32),
        ),
        in_specs=[pl.BlockSpec(memory_space=pltpu.HBM)] * 6,
        out_specs=(hbm,) * 5,
        scratch_shapes=scratch,
        compiler_params=pltpu.CompilerParams(
            collective_id=0, has_side_effects=True, vmem_limit_bytes=56 * 1024 * 1024
        ),
        cost_estimate=pl.CostEstimate(flops=3_600_000_000, bytes_accessed=7_000_000, transcendentals=500_000),
    )(x, c, cov, wd, wu, kern)


def hand_on(dec, gi, down, up, small, *rest):
    outs, held, sems = rest[:5], rest[5:10], rest[10]
    moves = []
    for n, source in enumerate((dec, gi, down, up, small)):
        parts = 4 if n < 2 else 1
        size = source.shape[0] // parts
        for k in range(parts):
            at = pl.ds(k * size, size)
            spot = 4 * n + k
            moves.append(
                (
                    pltpu.make_async_copy(source.at[at], held[n].at[at], sems.at[0, spot]),
                    pltpu.make_async_copy(held[n].at[at], outs[n].at[at], sems.at[1, spot]),
                )
            )
    for load, store in moves:
        load.start()
    for load, store in moves:
        load.wait()
        store.start()
    for load, store in moves:
        store.wait()


def handed_on(*arrays):
    hbm = pl.BlockSpec(memory_space=pltpu.HBM)
    return pl.pallas_call(
        hand_on,
        out_shape=tuple(jax.ShapeDtypeStruct(a.shape, a.dtype) for a in arrays),
        in_specs=[hbm] * len(arrays),
        out_specs=(hbm,) * len(arrays),
        scratch_shapes=[pltpu.VMEM(a.shape, a.dtype) for a in arrays]
        + [pltpu.SemaphoreType.DMA((2, 4 * len(arrays)))],
        compiler_params=pltpu.CompilerParams(vmem_limit_bytes=60 * 1024 * 1024),
    )(*arrays)


def shards(inputs, kernels, w_down, w_up, cotangent, coverage):
    total = inputs.shape[3] * inputs.shape[4] * N_LAT * N_LON
    scale = 1.0 / math.sqrt(total)
    found = level(
        inputs,
        cotangent,
        coverage,
        jnp.transpose(w_down, (0, 2, 1)),
        w_up,
        jnp.transpose(kernels, (1, 0, 2)),
        scale,
    )
    decoded, grad_input, down, up, small = handed_on(*found)
    return (
        decoded,
        grad_input,
        jnp.transpose(down.reshape(9, 64, 128), (0, 2, 1)),
        up.reshape(9, 64, 128),
        jnp.transpose(small, (0, 2, 1)),
    )


def solution(mesh):
    placed = (
        P(None, None, None, "lat", "lon"),
        P(),
        P(),
        P(),
        P(None, None, None, "lat", "lon"),
        P("lat", "lon"),
    )
    return jax.shard_map(
        shards,
        mesh=mesh,
        in_specs=placed,
        out_specs=(
            P(None, None, None, "lat", "lon"),
            P(None, None, None, "lat", "lon"),
            P(),
            P(),
            P(None, None, ("lat", "lon")),
        ),
        check_vma=False,
    )
```

time: 64.7 us -> 48 us (0.74)
  local copies, waits for them, and re-layouts: 13 us -> 0 us
  Pallas kernels: 50.7 us -> 47.3 us
    pallas_call x1, Pallas kernels: 50.7 us -> 43.9 us  [level(): pl.pallas_call(functools.partial(kernel, scale), out_shape=(planes, plane...]
    reshape x4 -> x0, local copies, waits for them, and re-layouts: 4.41 us -> none  [the longest x2 3.16 us: gathered(): return jnp.transpose(planes, (1, 2, 0, 3, 4)).reshape(2, 128, CELLS)]
    unnamed x15 -> x0, local copies, waits for them, and re-layouts: 4.38 us -> none
    transpose x3 -> x0, local copies, waits for them, and re-layouts: 4.15 us -> none  [the longest x1 2.2 us: spread(): return jnp.transpose(planes.reshape(2, 2, 64, ROWS, COLS), (2, 0, 1, 3, 4))]
    pallas_call x0 -> x1, Pallas kernels: none -> 3.33 us  [handed_on(): pl.pallas_call(hand_on, out_shape=tuple((jax.ShapeDtypeStruct(a.shape, a....]
where the time goes in v1:
time: 48 us; the launch traced here: 47.9 us
  Pallas kernels  47.3 us (99%)
  between operations  0.64 us (1%)
    pallas_call x1, Pallas kernels, level(): pl.pallas_call(functools.partial(kernel, scale), out_shape=(planes, plane...  43.9 us
    pallas_call x1, Pallas kernels, handed_on(): pl.pallas_call(hand_on, out_shape=tuple((jax.ShapeDtypeStruct(a.shape, a....  3.33 us

profile of v1, /device:TPU:1, one launch (start us, length us, event | category | flops | bytes accessed | tf_op | source)
XLA Modules:
  0.0 47.9 jit_solution(15836154005694608928)
XLA Ops:
  0.6 43.9 %shard_map.101 = (bf16[64,2,2,24,128]{4,3,2,1,0:T(8,128)(2,1)}, bf16[64,2,2,24,128]{4,3,2,1,0:T(8,128)(2,1)}, f32[576,128]{1,0:T(8,128)}, f32[576,128]{1,0:T(8,128)}, f32[2,1,9]{2,1,0:T(1,128)}) custom-call(bf16[64,2,2,24,128]{4,3,2,1,0:T(8,128)(2,1)} %x_hbm.1, bf16[64,2,2,24,128]{4,3,2,1,0:T(8,128)(2,1)} %c_hbm.1, s32[3,16]{1,0:T(4,128)} %cov_hbm.1, ...), custom_call_target="tpu_custom_call" | custom-call | flops 3600000000 | bytes 7000000 | tf_op jit(solution)/shard_map/pallas_call | solution.py:553
  44.6 3.3 %shard_map.102 = (bf16[64,2,2,24,128]{4,3,2,1,0:T(8,128)(2,1)}, bf16[64,2,2,24,128]{4,3,2,1,0:T(8,128)(2,1)}, f32[576,128]{1,0:T(8,128)}, f32[576,128]{1,0:T(8,128)}, f32[2,1,9]{2,1,0:T(1,128)}) custom-call(bf16[64,2,2,24,128]{4,3,2,1,0:T(8,128)(2,1)} %get-tuple-element.15.dec, bf16[64,2,2,24,128]{4,3,2,1,0:T(8,128)(2,1)} %get-tuple-element.16.gi, ...), custom_call_target="tpu_custom_call" | custom-call | tf_op jit(solution)/shard_map/pallas_call | solution.py:598

commit v2 on v1

--- a/solution.py
+++ b/solution.py
@@ -21,8 +21,10 @@
 MESH = pl.DeviceIdType.MESH
 N_LAT = 8
 N_LON = 16
-PIECE = 36
-PADDED = 48
+NEAR = 8
+FAR = 16
+PIECE = 72
+PADDED = 80
 
 
 def send(src, dst, send_sem, recv_sem, target):
@@ -38,11 +40,14 @@
 
 def greet(my_lat, my_lon):
     barrier = pltpu.get_barrier_semaphore()
-    peers = [(my_lat, lax.rem(my_lon + d, N_LON)) for d in range(1, N_LON)]
-    peers += [(lax.rem(my_lat + d, N_LAT), my_lon) for d in range(1, N_LAT)]
-    for down in (1, N_LAT - 1):
-        for side in (1, N_LON - 1):
-            peers.append((lax.rem(my_lat + down, N_LAT), lax.rem(my_lon + side, N_LON)))
+    run, place, rank = my_lon // NEAR, lax.rem(my_lon, NEAR), my_lat * 2 + my_lon // NEAR
+    peers = [(my_lat, run * NEAR + lax.rem(place + d, NEAR)) for d in range(1, NEAR)]
+    for d in range(1, FAR):
+        other = lax.rem(rank + d, FAR)
+        peers.append((other // 2, lax.rem(other, 2) * NEAR + place))
+    for side in (1, N_LON - 1):
+        beside = lax.rem(my_lon + side, N_LON)
+        peers += [(my_lat, beside), (lax.rem(my_lat + N_LAT - 1, N_LAT), beside)]
     for peer in peers:
         pl.semaphore_signal(barrier, inc=1, device_id=peer, device_id_type=MESH)
     return barrier, len(peers)
@@ -50,121 +55,77 @@
 
 class Sum:
     def __init__(self, my_lat, my_lon, pieces, got, part, parts, whole, *sems):
-        self.my_lat, self.my_lon = my_lat, my_lon
+        self.my_lat, self.run, self.place = my_lat, my_lon // NEAR, lax.rem(my_lon, NEAR)
+        self.rank = my_lat * 2 + self.run
         self.pieces, self.got, self.part, self.parts, self.whole = pieces, got, part, parts, whole
         self.s1, self.r1, self.s2, self.r2, self.s3, self.r3 = sems
 
-    def lon_peer(self, d):
-        return (self.my_lat, lax.rem(self.my_lon + d, N_LON))
-
-    def lat_peer(self, d):
-        return (lax.rem(self.my_lat + d, N_LAT), self.my_lon)
+    def near(self, d):
+        return (self.my_lat, self.run * NEAR + lax.rem(self.place + d, NEAR))
+
+    def far(self, d):
+        rank = lax.rem(self.rank + d, FAR)
+        return (rank // 2, lax.rem(rank, 2) * NEAR + self.place)
 
     def first(self, d):
-        peer = lax.rem(self.my_lon + d, N_LON)
-        return send(self.pieces.at[peer], self.got.at[d], self.s1, self.r1, self.lon_peer(d))
+        peer = lax.rem(self.place + d, NEAR)
+        return send(self.pieces.at[peer], self.got.at[d], self.s1, self.r1, self.near(d))
 
     def second(self, d):
-        return send(self.part, self.parts.at[d], self.s2, self.r2, self.lat_peer(d))
+        return send(self.part, self.parts.at[d], self.s2, self.r2, self.far(d))
 
     def third(self, d):
-        return send(self.part, self.whole.at[d], self.s3, self.r3, self.lon_peer(d))
+        return send(self.part, self.whole.at[d], self.s3, self.r3, self.near(d))
 
     def all_of(self, buffer, sent, received):
         arrived = buffer.at[pl.ds(1, buffer.shape[0] - 1)]
-        return send(arrived, arrived, sent, received, self.lon_peer(1))
+        return send(arrived, arrived, sent, received, self.near(1))
 
     def start_first(self):
-        for d in range(1, N_LON):
+        for d in range(1, NEAR):
             self.first(d).start()
 
     def start_second(self):
         self.all_of(self.got, self.s1, self.r1).wait_recv()
-        total = self.pieces[self.my_lon].astype(jnp.float32)
-        for d in range(1, N_LON):
-            total = total + self.got[d].astype(jnp.float32)
-        rounded = total.astype(jnp.bfloat16)
+        total = self.pieces[self.place].astype(F32)
+        for d in range(1, NEAR):
+            total = total + self.got[d].astype(F32)
+        rounded = total.astype(BF)
         self.part[...] = rounded
         self.parts[0] = rounded
-        for d in range(1, N_LAT):
+        for d in range(1, FAR):
             self.second(d).start()
 
     def start_third(self):
         self.all_of(self.parts, self.s2, self.r2).wait()
-        total = jnp.zeros((PADDED, 128), jnp.float32)
-        for lat in range(N_LAT):
-            slot = lax.rem(self.my_lat - lat + N_LAT, N_LAT)
-            total = total + self.parts[slot].astype(jnp.float32)
-        rounded = total.astype(jnp.bfloat16)
+        total = jnp.zeros((PADDED, 128), F32)
+        for rank in range(FAR):
+            total = total + self.parts[lax.rem(self.rank - rank + FAR, FAR)].astype(F32)
+        rounded = total.astype(BF)
         self.part[...] = rounded
         self.whole[0] = rounded
-        for d in range(1, N_LON):
+        for d in range(1, NEAR):
             self.third(d).start()
+
+    def extra(self, q):
+        return self.whole[lax.rem(self.place - q + NEAR, NEAR)].astype(F32)[PIECE:]
 
     def finish(self, scale, out):
         self.all_of(self.whole, self.s3, self.r3).wait_recv()
-        for d in range(N_LON):
-            k = lax.rem(self.my_lon - d + N_LON, N_LON)
-            piece = self.whole[d].astype(jnp.float32)[:PIECE] * scale
-            out[pl.ds(k * PIECE, PIECE), :] = piece
+        for d in range(NEAR):
+            k = lax.rem(self.place - d + NEAR, NEAR)
+            at = pl.ds(pl.multiple_of(k * PIECE, 8), PIECE)
+            out[at, :] = self.whole[d].astype(F32)[:PIECE] * scale
 
     def settle(self):
         self.all_of(self.got, self.s1, self.r1).wait_send()
         self.all_of(self.whole, self.s3, self.r3).wait_send()
 
 
-class Small(Sum):
-    def __init__(self, my_lat, my_lon, mine, got, part, parts, *sems):
-        self.my_lat, self.my_lon = my_lat, my_lon
-        self.mine, self.got, self.part, self.parts = mine, got, part, parts
-        self.s1, self.r1, self.s2, self.r2 = sems
-
-    def first(self, d):
-        return send(self.mine, self.got.at[d], self.s1, self.r1, self.lon_peer(d))
-
-    def start_second(self):
-        self.all_of(self.got, self.s1, self.r1).wait_recv()
-        total = self.mine[...]
-        for d in range(1, N_LON):
-            total = total + self.got[d]
-        self.part[...] = total
-        for d in range(1, N_LAT):
-            self.second(d).start()
-
-    def finish(self, scale, out):
-        self.all_of(self.parts, self.s2, self.r2).wait_recv()
-        total = self.part[...]
-        for d in range(1, N_LAT):
-            total = total + self.parts[d]
-        lane = lax.broadcasted_iota(jnp.int32, total.shape, 1)
-        mine = lane == self.my_lat * N_LON + self.my_lon
-        column = jnp.sum(jnp.where(mine, total, 0.0), axis=1, keepdims=True) * scale
-        row = lax.broadcasted_iota(jnp.int32, total.shape, 0)
-        for t in range(2):
-            line = jnp.sum(jnp.where(row == lane + 9 * t, column, 0.0), axis=0, keepdims=True)
-            out[t] = line[:, 0:9]
-
-    def settle(self):
-        self.all_of(self.got, self.s1, self.r1).wait_send()
-        self.all_of(self.parts, self.s2, self.r2).wait_send()
-
-
 def sum_scratch():
-    return [
-        pltpu.VMEM((N_LON, PADDED, 128), jnp.bfloat16),
-        pltpu.VMEM((N_LON, PADDED, 128), jnp.bfloat16),
-        pltpu.VMEM((PADDED, 128), jnp.bfloat16),
-        pltpu.VMEM((N_LAT, PADDED, 128), jnp.bfloat16),
-        pltpu.VMEM((N_LON, PADDED, 128), jnp.bfloat16),
-    ] + [pltpu.SemaphoreType.DMA] * 6
-
-
-def small_scratch(shape):
-    return [
-        pltpu.VMEM((N_LON,) + shape, jnp.float32),
-        pltpu.VMEM(shape, jnp.float32),
-        pltpu.VMEM((N_LAT,) + shape, jnp.float32),
-    ] + [pltpu.SemaphoreType.DMA] * 4
+    piece = lambda *lead: pltpu.VMEM(lead + (PADDED, 128), BF)
+    buffers = [piece(NEAR), piece(NEAR), piece(), piece(FAR), piece(NEAR)]
+    return buffers + [pltpu.SemaphoreType.DMA] * 6
 
 
 def row_at(i):
@@ -178,6 +139,15 @@
         target[mid:end, 0:128] = source[3 * a + 2]
         target[top:mid, 128:256] = jnp.zeros((64, 128), BF)
         target[mid:end, 128:256] = source[3 * a]
+
+
+def own_channel(total, channel, scale, out):
+    row = lax.broadcasted_iota(jnp.int32, total.shape, 0)
+    lane = lax.broadcasted_iota(jnp.int32, total.shape, 1)
+    column = jnp.sum(jnp.where(lane == channel, total, 0.0), axis=1, keepdims=True) * scale
+    for t in range(2):
+        line = jnp.sum(jnp.where(row == lane + 9 * t, column, 0.0), axis=0, keepdims=True)
+        out[t] = line[:, 0:9]
 
 
 def loop(low, high, body, wide=1):
@@ -218,7 +188,6 @@
     has_dn = (my_lat < N_LAT - 1).astype(F32)
     down = Sum(my_lat, my_lon, *sums[:11])
     up = Sum(my_lat, my_lon, *sums[11:22])
-    small = Small(my_lat, my_lon, small_mine, *sums[22:29])
 
     loads = []
     for n, (source, raw) in enumerate(((x_hbm, raw_x), (c_hbm, raw_c))):
@@ -423,14 +392,8 @@
             flat[(3 * a + 1) * 64 : (3 * a + 2) * 64, :] = grad[top:mid, 0:128]
             flat[(3 * a + 2) * 64 : (3 * a + 3) * 64, :] = grad[mid:end, 0:128]
             flat[3 * a * 64 : (3 * a + 1) * 64, :] = grad[mid:end, 128:256]
-        for k in range(N_LON):
+        for k in range(NEAR):
             total.pieces[k] = flat[pl.ds(k * PIECE, PADDED), :].astype(BF)
-        total.start_first()
-
-    flat[576:624, :] = jnp.zeros((48, 128), F32)
-    weight_grad(xa0, xa1, pg2, down)
-
-    weight_grad(ma0, ma1, d2, up)
 
     def kernel_grad(left, left_row, right, right_row, first_row):
         def step(i, accs):
@@ -446,10 +409,17 @@
         for t in range(9):
             small_mine[first_row + t : first_row + t + 1, :] = jnp.sum(accs[t], axis=0, keepdims=True)
 
+    flat[576:584, :] = jnp.zeros((8, 128), F32)
+    weight_grad(xa0, xa1, pg2, down)
+    down.start_first()
     small_mine[16:24, :] = jnp.zeros((8, 128), F32)
     kernel_grad(r1, 1, s0, 1, 0)
     kernel_grad(r2, 2, s1, 0, 9)
-    small.start_first()
+    weight_grad(ma0, ma1, d2, up)
+    for q in range(3):
+        rows = flat[q * PIECE : (q + 1) * PIECE, :], small_mine[q * 8 : (q + 1) * 8, :]
+        up.pieces[q] = jnp.concatenate(rows, axis=0).astype(BF)
+    up.start_first()
 
     def add_piece(weight, pairs, f0, f1, planes, n):
         at = pl.ds(pl.multiple_of(n * 512, 512), 512)
@@ -485,33 +455,33 @@
     gi_piece = functools.partial(add_piece, wdm, pg2, ma0, ma1, planes_c)
     below = pl.ds(CELLS, COLS)
 
+    down.start_second()
     loop(0, 3, dec_piece)
-    down.start_second()
+    up.start_second()
     for copy, field in zip(third, (pg2, d2)):
         copy.wait_recv()
         field[below, :] = field[below, :] * has_dn.astype(BF)
     loop(3, 6, dec_piece)
     stores = put_out(planes_x, raw_x, dec_hbm, out_sem)
-    up.start_second()
-    loop(0, 2, gi_piece)
     down.start_third()
-    small.start_second()
-    loop(2, 4, gi_piece)
+    loop(0, 4, gi_piece)
     up.start_third()
     loop(4, 6, gi_piece)
     stores += put_out(planes_c, raw_c, gi_hbm, out_sem.at[pl.ds(4, 4)])
     down.finish(scale, down_out)
     stores.append(pltpu.make_async_copy(down_out, down_hbm, out_sem.at[8]))
     stores[-1].start()
-    small.finish(scale, small_out)
-    stores.append(pltpu.make_async_copy(small_out, small_hbm, out_sem.at[9]))
-    stores[-1].start()
     up.finish(scale, up_out)
     stores.append(pltpu.make_async_copy(up_out, up_hbm, out_sem.at[10]))
     stores[-1].start()
+    for q in range(3):
+        small_mine[q * 8 : (q + 1) * 8, :] = up.extra(q)
+    own_channel(small_mine[...], my_lat * N_LON + my_lon, scale, small_out)
+    stores.append(pltpu.make_async_copy(small_out, small_hbm, out_sem.at[9]))
+    stores[-1].start()
     for copy in first + second + third:
         copy.wait_send()
-    for each in (down, up, small):
+    for each in (down, up):
         each.settle()
     for store in stores:
         store.wait()
@@ -544,11 +514,10 @@
         + [mat(128)] * 2
         + [pltpu.VMEM((200, 128), F32)] * 2
         + [mat(576)] * 4
-        + [pltpu.VMEM((384, 256), F32), pltpu.VMEM((624, 128), F32), pltpu.VMEM((24, 128), F32)]
+        + [pltpu.VMEM((384, 256), F32), pltpu.VMEM((584, 128), F32), pltpu.VMEM((24, 128), F32)]
         + [dma(12), dma(11), dma(6), dma(6), dma(2), dma(2), dma(2), dma(2)]
         + sum_scratch()
         + sum_scratch()
-        + small_scratch((24, 128))
     )
     return pl.pallas_call(
         functools.partial(kernel, scale),
@@ -563,46 +532,35 @@
         out_specs=(hbm,) * 5,
         scratch_shapes=scratch,
         compiler_params=pltpu.CompilerParams(
-            collective_id=0, has_side_effects=True, vmem_limit_bytes=56 * 1024 * 1024
+            collective_id=0, has_side_effects=True, vmem_limit_bytes=46 * 1024 * 1024
         ),
         cost_estimate=pl.CostEstimate(flops=3_600_000_000, bytes_accessed=7_000_000, transcendentals=500_000),
-    )(x, c, cov, wd, wu, kern)
-
-
-def hand_on(dec, gi, down, up, small, *rest):
-    outs, held, sems = rest[:5], rest[5:10], rest[10]
-    moves = []
-    for n, source in enumerate((dec, gi, down, up, small)):
-        parts = 4 if n < 2 else 1
-        size = source.shape[0] // parts
-        for k in range(parts):
-            at = pl.ds(k * size, size)
-            spot = 4 * n + k
-            moves.append(
-                (
-                    pltpu.make_async_copy(source.at[at], held[n].at[at], sems.at[0, spot]),
-                    pltpu.make_async_copy(held[n].at[at], outs[n].at[at], sems.at[1, spot]),
-                )
-            )
-    for load, store in moves:
-        load.start()
-    for load, store in moves:
-        load.wait()
-        store.start()
-    for load, store in moves:
-        store.wait()
+    )(*(pltpu.with_memory_space_constraint(v, pltpu.HBM) for v in (x, c, cov, wd, wu, kern)))
+
+
+def hand_on(*refs):
+    count = len(refs) // 2
+    sems = refs[-1]
+    copies = [
+        pltpu.make_async_copy(source, target, sems.at[n])
+        for n, (source, target) in enumerate(zip(refs[:count], refs[count : 2 * count]))
+    ]
+    for copy in copies:
+        copy.start()
+    for copy in copies:
+        copy.wait()
 
 
 def handed_on(*arrays):
+    vmem = pl.BlockSpec(memory_space=pltpu.VMEM)
     hbm = pl.BlockSpec(memory_space=pltpu.HBM)
     return pl.pallas_call(
         hand_on,
         out_shape=tuple(jax.ShapeDtypeStruct(a.shape, a.dtype) for a in arrays),
-        in_specs=[hbm] * len(arrays),
+        in_specs=[vmem] * len(arrays),
         out_specs=(hbm,) * len(arrays),
-        scratch_shapes=[pltpu.VMEM(a.shape, a.dtype) for a in arrays]
-        + [pltpu.SemaphoreType.DMA((2, 4 * len(arrays)))],
-        compiler_params=pltpu.CompilerParams(vmem_limit_bytes=60 * 1024 * 1024),
+        scratch_shapes=[pltpu.SemaphoreType.DMA((len(arrays),))],
+        compiler_params=pltpu.CompilerParams(vmem_limit_bytes=16 * 1024 * 1024),
     )(*arrays)
 
 

time: 48 us -> 45.2 us (0.942)
  Pallas kernels: 47.3 us -> 44.5 us
    pallas_call x1, Pallas kernels: 3.33 us -> 1.9 us  [handed_on(): pl.pallas_call(hand_on, out_shape=tuple((jax.ShapeDtypeStruct(a.shape, a....]
    pallas_call x1, Pallas kernels: 43.9 us -> 42.6 us  [level(): pl.pallas_call(functools.partial(kernel, scale), out_shape=(planes, plane...]
where the time goes in v2:
time: 45.2 us; the launch traced here: 45.1 us
  Pallas kernels  44.5 us (98%)
  between operations  0.64 us (1%)
    pallas_call x1, Pallas kernels, level(): pl.pallas_call(functools.partial(kernel, scale), out_shape=(planes, plane...  42.6 us
    pallas_call x1, Pallas kernels, handed_on(): pl.pallas_call(hand_on, out_shape=tuple((jax.ShapeDtypeStruct(a.shape, a....  1.9 us

profile of v2, /device:TPU:1, one launch (start us, length us, event | category | flops | bytes accessed | tf_op | source)
XLA Modules:
  0.0 45.1 jit_solution(4803613388395565642)
XLA Ops:
  0.6 42.6 %shard_map.101 = (bf16[64,2,2,24,128]{4,3,2,1,0:T(8,128)(2,1)S(1)}, bf16[64,2,2,24,128]{4,3,2,1,0:T(8,128)(2,1)S(1)}, f32[576,128]{1,0:T(8,128)S(1)}, f32[576,128]{1,0:T(8,128)S(1)}, f32[2,1,9]{2,1,0:T(1,128)S(1)}) custom-call(bf16[64,2,2,24,128]{4,3,2,1,0:T(8,128)(2,1)} %x_hbm.1, bf16[64,2,2,24,128]{4,3,2,1,0:T(8,128)(2,1)} %c_hbm.1, s32[3,16]{1,0:T(4,128)} %cov_hbm.1, ...), custom_call_target="tpu_custom_call" | custom-call | flops 3600000000 | bytes 7000000 | tf_op jit(solution)/shard_map/pallas_call | solution.py:522
  43.2 1.9 %shard_map.102 = (bf16[64,2,2,24,128]{4,3,2,1,0:T(8,128)(2,1)}, bf16[64,2,2,24,128]{4,3,2,1,0:T(8,128)(2,1)}, f32[576,128]{1,0:T(8,128)}, f32[576,128]{1,0:T(8,128)}, f32[2,1,9]{2,1,0:T(1,128)}) custom-call(bf16[64,2,2,24,128]{4,3,2,1,0:T(8,128)(2,1)S(1)} %get-tuple-element.15.refs_0_, bf16[64,2,2,24,128]{4,3,2,1,0:T(8,128)(2,1)S(1)} %get-tuple-element.16.refs_1_, ...), custom_call_target="tpu_custom_call" | custom-call | tf_op jit(solution)/shard_map/pallas_call | solution.py:557

commit v3 on v2

--- a/solution.py
+++ b/solution.py
@@ -163,13 +163,14 @@
     return pl.ds(i, 64, stride=ROWS)
 
 
-def taps_sum(field, row, base, coefs, first, rows_of, cols_of, span):
-    acc = field[row, pl.ds(base, span), :]
+def taps_sum(field, coefs, first, rows_of, cols_of, span):
+    total = None
     for a in range(3):
         for b in range(3):
             coef = coefs[3 * a + b, first : first + 1, :]
-            acc = acc + coef * field[rows_of(a), pl.ds(cols_of(b), span), :]
-    return acc
+            term = coef * field[rows_of(a), pl.ds(cols_of(b), span), :]
+            total = term if total is None else total + term
+    return total
 
 
 def kernel(
@@ -208,6 +209,7 @@
     barrier, met = greet(my_lat, my_lon)
     for load in params:
         load.wait()
+    kern[4] = kern[4] + 1.0
     lay_weights(wd, wdm)
     lay_weights(wu, wum)
     spread = (
@@ -329,11 +331,11 @@
     loop(2, ROWS - 2, rims, 4)
 
     def forward_1(r):
-        acc = taps_sum(s0, r + 1, LO, kern, 0, lambda a: r + a, lambda b: LO - 1 + b, SPAN)
+        acc = taps_sum(s0, kern, 0, lambda a: r + a, lambda b: LO - 1 + b, SPAN)
         s1[r, pl.ds(LO, SPAN), :] = acc
 
     def backward_1(r):
-        acc = taps_sum(r2, r + 1, LO, kern, 1, lambda a: r - a + 2, lambda b: LO + 1 - b, SPAN)
+        acc = taps_sum(r2, kern, 1, lambda a: r - a + 2, lambda b: LO + 1 - b, SPAN)
         r1[r, pl.ds(LO, SPAN), :] = acc
 
     loop(2, ROWS, forward_1, 2)
@@ -346,16 +348,29 @@
         into[here, 128:256] = tmp[slot, 1 : COLS + 1, :].astype(BF)
 
     def backward_0(i):
-        acc = taps_sum(r1, i + 1, OFF, kern, 0, lambda a: i - a + 2, lambda b: OFF + 1 - b, REACH)
+        acc = taps_sum(r1, kern, 0, lambda a: i - a + 2, lambda b: OFF + 1 - b, REACH)
         value = acc.astype(BF).astype(F32) * ds_[i, pl.ds(OFF, REACH), :]
         pair(value, 0, pg2, i)
 
     def forward_0(i):
-        acc = taps_sum(s1, i + 1, OFF, kern, 1, lambda a: i + a, lambda b: OFF - 1 + b, REACH)
+        acc = taps_sum(s1, kern, 1, lambda a: i + a, lambda b: OFF - 1 + b, REACH)
         pair(acc, 2, d2, i)
 
     loop(2, ROWS - 2, backward_0, 2)
-    loop(2, ROWS - 2, forward_0, 2)
+    grad[...] = jnp.zeros_like(grad)
+
+    def add_grad(a0, a1, pairs, row, count):
+        at = pl.ds(pl.multiple_of(row * COLS, COLS), count * COLS)
+        after = pl.ds(pl.multiple_of((row + 1) * COLS, COLS), count * COLS)
+        taps = jnp.concatenate([a1[:, at], a0[:, at], a1[:, after]], axis=0)
+        grad[...] += jnp.dot(taps, pairs[at, :], preferred_element_type=F32)
+
+    def forward_and_grad(n):
+        add_grad(xa0, xa1, pg2, 4 + 4 * n, 4)
+        for k in range(5):
+            forward_0(2 + 5 * n + k)
+
+    loop(0, 4, forward_and_grad)
     for copy in second:
         copy.wait_recv()
     for n, field in enumerate((s0, r2)):
@@ -377,16 +392,8 @@
         send(pg2.at[pl.ds(0, COLS)], pg2.at[pl.ds(CELLS, COLS)], e3_s.at[0], e3_r.at[0], (up_lat, my_lon)),
         send(d2.at[pl.ds(0, COLS)], d2.at[pl.ds(CELLS, COLS)], e3_s.at[1], e3_r.at[1], (up_lat, my_lon)),
     ]
-    for copy in third:
-        copy.start()
-
-    def weight_grad(a0, a1, pairs, total):
-        half = CELLS // 2
-        for n in range(2):
-            at, after = pl.ds(n * half, half), pl.ds(n * half + COLS, half)
-            taps = jnp.concatenate([a1[:, at], a0[:, at], a1[:, after]], axis=0)
-            part = jnp.dot(taps, pairs[at, :], preferred_element_type=F32)
-            grad[...] = part if n == 0 else grad[...] + part
+
+    def lay_pieces(total):
         for a in range(3):
             top, mid, end = a * 128, a * 128 + 64, a * 128 + 128
             flat[(3 * a + 1) * 64 : (3 * a + 2) * 64, :] = grad[top:mid, 0:128]
@@ -395,27 +402,39 @@
         for k in range(NEAR):
             total.pieces[k] = flat[pl.ds(k * PIECE, PADDED), :].astype(BF)
 
-    def kernel_grad(left, left_row, right, right_row, first_row):
-        def step(i, accs):
-            own = left[i + left_row, OFF : OFF + COLS, :]
-            found = []
-            for a in range(3):
-                for b in range(3):
-                    other = right[i + a + right_row, pl.ds(OFF - 1 + b, COLS), :]
-                    found.append(accs[3 * a + b] + jnp.sum((own * other).reshape(16, 8, 128), axis=0))
-            return tuple(found)
-
-        accs = lax.fori_loop(0, ROWS, step, tuple(jnp.zeros((8, 128), F32) for _ in range(9)))
-        for t in range(9):
-            small_mine[first_row + t : first_row + t + 1, :] = jnp.sum(accs[t], axis=0, keepdims=True)
-
     flat[576:584, :] = jnp.zeros((8, 128), F32)
-    weight_grad(xa0, xa1, pg2, down)
+    small_mine[16:24, :] = jnp.zeros((8, 128), F32)
+    add_grad(xa0, xa1, pg2, 0, 4)
+    add_grad(xa0, xa1, pg2, ROWS - 4, 4)
+    lay_pieces(down)
     down.start_first()
-    small_mine[16:24, :] = jnp.zeros((8, 128), F32)
-    kernel_grad(r1, 1, s0, 1, 0)
-    kernel_grad(r2, 2, s1, 0, 9)
-    weight_grad(ma0, ma1, d2, up)
+    for copy in third:
+        copy.start()
+
+    def kernel_terms(own, other, accs):
+        found = []
+        for a in range(3):
+            for b in range(3):
+                near_by = other(a)[pl.ds(OFF - 1 + b, COLS), :]
+                found.append(accs[3 * a + b] + jnp.sum((own * near_by).reshape(16, 8, 128), axis=0))
+        return found
+
+    def up_step(n, accs):
+        add_grad(ma0, ma1, d2, 8 * n, 8)
+        accs = list(accs)
+        for k in range(8):
+            i = 8 * n + k
+            own = r1[i + 1, OFF : OFF + COLS, :]
+            accs[:9] = kernel_terms(own, lambda a: s0.at[i + a + 1], accs[:9])
+            own = r2[i + 2, OFF : OFF + COLS, :]
+            accs[9:] = kernel_terms(own, lambda a: s1.at[i + a], accs[9:])
+        return tuple(accs)
+
+    grad[...] = jnp.zeros_like(grad)
+    accs = lax.fori_loop(0, 3, up_step, tuple(jnp.zeros((8, 128), F32) for _ in range(18)))
+    for t in range(18):
+        small_mine[t : t + 1, :] = jnp.sum(accs[t], axis=0, keepdims=True)
+    lay_pieces(up)
     for q in range(3):
         rows = flat[q * PIECE : (q + 1) * PIECE, :], small_mine[q * 8 : (q + 1) * 8, :]
         up.pieces[q] = jnp.concatenate(rows, axis=0).astype(BF)
@@ -455,19 +474,18 @@
     gi_piece = functools.partial(add_piece, wdm, pg2, ma0, ma1, planes_c)
     below = pl.ds(CELLS, COLS)
 
+    loop(0, 1, dec_piece)
     down.start_second()
-    loop(0, 3, dec_piece)
-    up.start_second()
     for copy, field in zip(third, (pg2, d2)):
         copy.wait_recv()
         field[below, :] = field[below, :] * has_dn.astype(BF)
-    loop(3, 6, dec_piece)
+    loop(1, 6, dec_piece)
     stores = put_out(planes_x, raw_x, dec_hbm, out_sem)
+    up.start_second()
+    loop(0, 6, gi_piece)
+    stores += put_out(planes_c, raw_c, gi_hbm, out_sem.at[pl.ds(4, 4)])
     down.start_third()
-    loop(0, 4, gi_piece)
     up.start_third()
-    loop(4, 6, gi_piece)
-    stores += put_out(planes_c, raw_c, gi_hbm, out_sem.at[pl.ds(4, 4)])
     down.finish(scale, down_out)
     stores.append(pltpu.make_async_copy(down_out, down_hbm, out_sem.at[8]))
     stores[-1].start()

time: 45.2 us -> 44.5 us (0.985)
  Pallas kernels: 44.5 us -> 43.8 us
    pallas_call x1, Pallas kernels: 42.6 us -> 41.9 us  [level(): pl.pallas_call(functools.partial(kernel, scale), out_shape=(planes, plane...]
where the time goes in v3:
time: 44.5 us; the launch traced here: 44.4 us
  Pallas kernels  43.8 us (98%)
  between operations  0.64 us (1%)
    pallas_call x1, Pallas kernels, level(): pl.pallas_call(functools.partial(kernel, scale), out_shape=(planes, plane...  41.9 us
    pallas_call x1, Pallas kernels, handed_on(): pl.pallas_call(hand_on, out_shape=tuple((jax.ShapeDtypeStruct(a.shape, a....  1.9 us

profile of v3, /device:TPU:1, one launch (start us, length us, event | category | flops | bytes accessed | tf_op | source)
XLA Modules:
  0.0 44.4 jit_solution(16862640031831603574)
XLA Ops:
  0.6 41.9 %shard_map.101 = (bf16[64,2,2,24,128]{4,3,2,1,0:T(8,128)(2,1)S(1)}, bf16[64,2,2,24,128]{4,3,2,1,0:T(8,128)(2,1)S(1)}, f32[576,128]{1,0:T(8,128)S(1)}, f32[576,128]{1,0:T(8,128)S(1)}, f32[2,1,9]{2,1,0:T(1,128)S(1)}) custom-call(bf16[64,2,2,24,128]{4,3,2,1,0:T(8,128)(2,1)} %x_hbm.1, bf16[64,2,2,24,128]{4,3,2,1,0:T(8,128)(2,1)} %c_hbm.1, s32[3,16]{1,0:T(4,128)} %cov_hbm.1, ...), custom_call_target="tpu_custom_call" | custom-call | flops 3600000000 | bytes 7000000 | tf_op jit(solution)/shard_map/pallas_call | solution.py:540
  42.5 1.9 %shard_map.102 = (bf16[64,2,2,24,128]{4,3,2,1,0:T(8,128)(2,1)}, bf16[64,2,2,24,128]{4,3,2,1,0:T(8,128)(2,1)}, f32[576,128]{1,0:T(8,128)}, f32[576,128]{1,0:T(8,128)}, f32[2,1,9]{2,1,0:T(1,128)}) custom-call(bf16[64,2,2,24,128]{4,3,2,1,0:T(8,128)(2,1)S(1)} %get-tuple-element.15.refs_0_, bf16[64,2,2,24,128]{4,3,2,1,0:T(8,128)(2,1)S(1)} %get-tuple-element.16.refs_1_, ...), custom_call_target="tpu_custom_call" | custom-call | tf_op jit(solution)/shard_map/pallas_call | solution.py:575

commit v4 on v3

--- a/solution.py
+++ b/solution.py
@@ -244,14 +244,14 @@
         for v in range(2):
             loads[2 * u + v].wait()
             unfold(raw_x, planes_x, 2 * u + v)
-        loop(0, ROWS, functools.partial(turn, u, None, planes_x, field, into, 0), 4)
+        loop(0, ROWS, functools.partial(turn, u, None, planes_x, field, into, 0), 12)
     for u, field, into in ((0, ma0, mb0), (1, ma1, mb1)):
         for v in range(2):
             loads[4 + 2 * u + v].wait()
             unfold(raw_c, planes_c, 2 * u + v)
         for q in range(3):
             body = functools.partial(turn, u, flags[q : q + 1, :], planes_c, field, into, 4)
-            loop(8 * q, 8 * q + 8, body, 4)
+            loop(8 * q, 8 * q + 8, body, 8)
     send_l[...] = pack_l[...].astype(BF)
     send_r[...] = pack_r[...].astype(BF)
 
@@ -278,8 +278,6 @@
             for k in range(count):
                 y[i + k, OFF : OFF + COLS, :] = found[k * COLS : (k + 1) * COLS]
 
-    conv_rows(1, 3)
-    loop(1, ROWS // 4, lambda n: conv_rows(4 * n, 4))
 
     def activate(i, low=LO, count=SPAN):
         span, before = pl.ds(low, count), pl.ds(low - 1, count)
@@ -294,8 +292,31 @@
         activate(i, LO, 16)
         activate(i, OFF + COLS, 8)
 
-    loop(1, ROWS - 1, activate, 2)
-    activate(ROWS - 1)
+    def activate_and_conv(n):
+        for k in range(4):
+            activate(4 * n - 4 + k)
+        conv_rows(4 * n, 4)
+
+    conv_rows(1, 3)
+    loop(1, ROWS // 4, activate_and_conv)
+    loop(ROWS - 4, ROWS, activate, 4)
+
+    def forward_1(r, low=LO, count=SPAN):
+        acc = taps_sum(s0, kern, 0, lambda a: r + a, lambda b: low - 1 + b, count)
+        s1[r, pl.ds(low, count), :] = acc
+
+    def backward_1(r, low=LO, count=SPAN):
+        acc = taps_sum(r2, kern, 1, lambda a: r - a + 2, lambda b: low + 1 - b, count)
+        r1[r, pl.ds(low, count), :] = acc
+
+    def mend(r):
+        for step in (forward_1, backward_1):
+            step(r, LO, 16)
+            step(r, LO + SPAN - 16, 16)
+
+    loop(3, ROWS - 1, forward_1, 2)
+    loop(3, ROWS - 1, backward_1, 2)
+
 
     for copy in first:
         copy.wait_recv()
@@ -330,16 +351,11 @@
         copy.start()
     loop(2, ROWS - 2, rims, 4)
 
-    def forward_1(r):
-        acc = taps_sum(s0, kern, 0, lambda a: r + a, lambda b: LO - 1 + b, SPAN)
-        s1[r, pl.ds(LO, SPAN), :] = acc
-
-    def backward_1(r):
-        acc = taps_sum(r2, kern, 1, lambda a: r - a + 2, lambda b: LO + 1 - b, SPAN)
-        r1[r, pl.ds(LO, SPAN), :] = acc
-
-    loop(2, ROWS, forward_1, 2)
-    loop(2, ROWS, backward_1, 2)
+    loop(3, ROWS - 1, mend, 2)
+    for r in (2, ROWS - 1):
+        forward_1(r)
+        backward_1(r)
+
     def pair(value, slot, into, i):
         slot = slot + lax.rem(i, 2)
         tmp[slot, 0:REACH, :] = value
@@ -378,16 +394,16 @@
             at = pl.ds(n * 288 + k * SPAN, SPAN)
             field[k, LO : LO + SPAN, :] = got_dn[at, :].astype(F32) * has_up
             field[ROWS + 2 + k, LO : LO + SPAN, :] = got_up[at, :].astype(F32) * has_dn
-    for r in (0, 1, ROWS, ROWS + 1):
-        forward_1(r)
-        backward_1(r)
-    for field in (s1, r1):
+    def bound(field):
         field[0, LO : LO + SPAN, :] = field[0, LO : LO + SPAN, :] * has_up
         field[ROWS + 1, LO : LO + SPAN, :] = field[ROWS + 1, LO : LO + SPAN, :] * has_dn
 
+    for r in (0, 1, ROWS, ROWS + 1):
+        backward_1(r)
+    bound(r1)
+
     for i in (0, 1, ROWS - 2, ROWS - 1):
         backward_0(i)
-        forward_0(i)
     third = [
         send(pg2.at[pl.ds(0, COLS)], pg2.at[pl.ds(CELLS, COLS)], e3_s.at[0], e3_r.at[0], (up_lat, my_lon)),
         send(d2.at[pl.ds(0, COLS)], d2.at[pl.ds(CELLS, COLS)], e3_s.at[1], e3_r.at[1], (up_lat, my_lon)),
@@ -408,6 +424,11 @@
     add_grad(xa0, xa1, pg2, ROWS - 4, 4)
     lay_pieces(down)
     down.start_first()
+    for r in (0, 1, ROWS, ROWS + 1):
+        forward_1(r)
+    bound(s1)
+    for i in (0, 1, ROWS - 2, ROWS - 1):
+        forward_0(i)
     for copy in third:
         copy.start()
 

time: 44.5 us -> 43.5 us (0.978)
  Pallas kernels: 43.8 us -> 42.7 us
    pallas_call x1, Pallas kernels: 41.9 us -> 40.8 us  [level(): pl.pallas_call(functools.partial(kernel, scale), out_shape=(planes, plane...]
where the time goes in v4:
time: 43.5 us; the launch traced here: 43.4 us
  Pallas kernels  42.7 us (98%)
  between operations  0.64 us (1%)
    pallas_call x1, Pallas kernels, level(): pl.pallas_call(functools.partial(kernel, scale), out_shape=(planes, plane...  40.8 us
    pallas_call x1, Pallas kernels, handed_on(): pl.pallas_call(hand_on, out_shape=tuple((jax.ShapeDtypeStruct(a.shape, a....  1.9 us

profile of v4, /device:TPU:1, one launch (start us, length us, event | category | flops | bytes accessed | tf_op | source)
XLA Modules:
  0.0 43.4 jit_solution(8848841133245841306)
XLA Ops:
  0.6 40.8 %shard_map.101 = (bf16[64,2,2,24,128]{4,3,2,1,0:T(8,128)(2,1)S(1)}, bf16[64,2,2,24,128]{4,3,2,1,0:T(8,128)(2,1)S(1)}, f32[576,128]{1,0:T(8,128)S(1)}, f32[576,128]{1,0:T(8,128)S(1)}, f32[2,1,9]{2,1,0:T(1,128)S(1)}) custom-call(bf16[64,2,2,24,128]{4,3,2,1,0:T(8,128)(2,1)} %x_hbm.1, bf16[64,2,2,24,128]{4,3,2,1,0:T(8,128)(2,1)} %c_hbm.1, s32[3,16]{1,0:T(4,128)} %cov_hbm.1, ...), custom_call_target="tpu_custom_call" | custom-call | flops 3600000000 | bytes 7000000 | tf_op jit(solution)/shard_map/pallas_call | solution.py:561
  41.5 1.9 %shard_map.102 = (bf16[64,2,2,24,128]{4,3,2,1,0:T(8,128)(2,1)}, bf16[64,2,2,24,128]{4,3,2,1,0:T(8,128)(2,1)}, f32[576,128]{1,0:T(8,128)}, f32[576,128]{1,0:T(8,128)}, f32[2,1,9]{2,1,0:T(1,128)}) custom-call(bf16[64,2,2,24,128]{4,3,2,1,0:T(8,128)(2,1)S(1)} %get-tuple-element.15.refs_0_, bf16[64,2,2,24,128]{4,3,2,1,0:T(8,128)(2,1)S(1)} %get-tuple-element.16.refs_1_, ...), custom_call_target="tpu_custom_call" | custom-call | tf_op jit(solution)/shard_map/pallas_call | solution.py:596

commit v5 on v4

--- a/solution.py
+++ b/solution.py
@@ -495,17 +495,19 @@
     gi_piece = functools.partial(add_piece, wdm, pg2, ma0, ma1, planes_c)
     below = pl.ds(CELLS, COLS)
 
-    loop(0, 1, dec_piece)
+    loop(0, 2, dec_piece)
     down.start_second()
+    loop(2, 5, dec_piece)
+    up.start_second()
     for copy, field in zip(third, (pg2, d2)):
         copy.wait_recv()
         field[below, :] = field[below, :] * has_dn.astype(BF)
-    loop(1, 6, dec_piece)
+    loop(5, 6, dec_piece)
     stores = put_out(planes_x, raw_x, dec_hbm, out_sem)
-    up.start_second()
-    loop(0, 6, gi_piece)
+    loop(0, 4, gi_piece)
+    down.start_third()
+    loop(4, 6, gi_piece)
     stores += put_out(planes_c, raw_c, gi_hbm, out_sem.at[pl.ds(4, 4)])
-    down.start_third()
     up.start_third()
     down.finish(scale, down_out)
     stores.append(pltpu.make_async_copy(down_out, down_hbm, out_sem.at[8]))
@@ -580,10 +582,13 @@
 def hand_on(*refs):
     count = len(refs) // 2
     sems = refs[-1]
-    copies = [
-        pltpu.make_async_copy(source, target, sems.at[n])
-        for n, (source, target) in enumerate(zip(refs[:count], refs[count : 2 * count]))
-    ]
+    copies = []
+    for n, (source, target) in enumerate(zip(refs[:count], refs[count : 2 * count])):
+        parts = 4 if n < 2 else 1
+        size = source.shape[0] // parts
+        for k in range(parts):
+            at = pl.ds(k * size, size)
+            copies.append(pltpu.make_async_copy(source.at[at], target.at[at], sems.at[4 * n + k]))
     for copy in copies:
         copy.start()
     for copy in copies:
@@ -598,7 +603,7 @@
         out_shape=tuple(jax.ShapeDtypeStruct(a.shape, a.dtype) for a in arrays),
         in_specs=[vmem] * len(arrays),
         out_specs=(hbm,) * len(arrays),
-        scratch_shapes=[pltpu.SemaphoreType.DMA((len(arrays),))],
+        scratch_shapes=[pltpu.SemaphoreType.DMA((4 * len(arrays),))],
         compiler_params=pltpu.CompilerParams(vmem_limit_bytes=16 * 1024 * 1024),
     )(*arrays)
 

time: 43.5 us -> 43.6 us (level)
  no operation moved by 1% of the time
where the time goes in v5:
time: 43.6 us; the launch traced here: 43.5 us
  Pallas kernels  42.9 us (98%)
  between operations  0.64 us (1%)
    pallas_call x1, Pallas kernels, level(): pl.pallas_call(functools.partial(kernel, scale), out_shape=(planes, plane...  40.8 us
    pallas_call x1, Pallas kernels, handed_on(): pl.pallas_call(hand_on, out_shape=tuple((jax.ShapeDtypeStruct(a.shape, a....  2.03 us

profile of v5, /device:TPU:1, one launch (start us, length us, event | category | flops | bytes accessed | tf_op | source)
XLA Modules:
  0.0 43.5 jit_solution(17123790860195830579)
XLA Ops:
  0.6 40.8 %shard_map.101 = (bf16[64,2,2,24,128]{4,3,2,1,0:T(8,128)(2,1)S(1)}, bf16[64,2,2,24,128]{4,3,2,1,0:T(8,128)(2,1)S(1)}, f32[576,128]{1,0:T(8,128)S(1)}, f32[576,128]{1,0:T(8,128)S(1)}, f32[2,1,9]{2,1,0:T(1,128)S(1)}) custom-call(bf16[64,2,2,24,128]{4,3,2,1,0:T(8,128)(2,1)} %x_hbm.1, bf16[64,2,2,24,128]{4,3,2,1,0:T(8,128)(2,1)} %c_hbm.1, s32[3,16]{1,0:T(4,128)} %cov_hbm.1, ...), custom_call_target="tpu_custom_call" | custom-call | flops 3600000000 | bytes 7000000 | tf_op jit(solution)/shard_map/pallas_call | solution.py:563
  41.5 2.0 %shard_map.102 = (bf16[64,2,2,24,128]{4,3,2,1,0:T(8,128)(2,1)}, bf16[64,2,2,24,128]{4,3,2,1,0:T(8,128)(2,1)}, f32[576,128]{1,0:T(8,128)}, f32[576,128]{1,0:T(8,128)}, f32[2,1,9]{2,1,0:T(1,128)}) custom-call(bf16[64,2,2,24,128]{4,3,2,1,0:T(8,128)(2,1)S(1)} %get-tuple-element.15.refs_0_, bf16[64,2,2,24,128]{4,3,2,1,0:T(8,128)(2,1)S(1)} %get-tuple-element.16.refs_1_, ...), custom_call_target="tpu_custom_call" | custom-call | tf_op jit(solution)/shard_map/pallas_call | solution.py:601
